TPU v7x, 32 devices: a whole 2x2x4 slice. The times are simulated.
32 devices in a mesh: pipe: 2 (over core), dp: 4 (over y, x), expert: 4 (over z).
Axes of the slice: x: 2, y: 2, z: 4, core: 2. Of those that a mesh axis runs over, the one named last changes fastest.
Arguments:
- inputs: bfloat16 [2, 16, 64, 1024], P(None, ('dp', 'expert')), may hold values from -6 to 6
- cotangent: bfloat16 [2, 16, 64, 1024], P(None, ('dp', 'expert')), may hold values from -6 to 6
- segments: int32 [2, 16, 64], P(None, ('dp', 'expert')), may hold values from 0 to 3, never falling along the last dimension, each value on 1 to 32 neighbouring positions
- routes: int32 [2, 2, 16, 64, 8], P('pipe', None, ('dp', 'expert')), may hold values from 0 to 31, all different within a row; in each aligned block of 64 rows (0 to 63, 64 to 127, ..., all dimensions but the last counted through in order) at most 20 rows name the same one
- norm_attn: float32 [2, 1024], P('pipe'), may hold values from 0.5 to 1.5
- w_query: bfloat16 [2, 1024, 1024], P('pipe', 'dp'), may hold values from -0.1875 to 0.1875
- key_value_weight: bfloat16 [2, 1024, 1024], P('pipe', 'dp'), may hold values from -0.1875 to 0.1875
- w_out: bfloat16 [2, 1024, 1024], P('pipe', 'dp'), may hold values from -0.75 to 0.75
- norm_ffn: float32 [2, 1024], P('pipe'), may hold values from 0.5 to 1.5
- w_router: bfloat16 [2, 1024, 32], P('pipe'), may hold values from -0.09375 to 0.09375
- w_gate: bfloat16 [2, 32, 1024, 512], P('pipe', 'expert'), may hold values from -0.1875 to 0.1875
- w_up: bfloat16 [2, 32, 1024, 512], P('pipe', 'expert'), may hold values from -0.1875 to 0.1875
- w_down: bfloat16 [2, 32, 512, 1024], P('pipe', 'expert'), may hold values from -1 to 1
Outputs:
- hidden: float32 [2, 2, 16, 64, 1024], P('pipe', None, ('dp', 'expert'))
- grad_input: float32 [2, 2, 16, 64, 1024], P('pipe', None, ('dp', 'expert'))
- g_norm_attn: float32 [2, 1024], P('pipe', 'dp')
- g_query: float32 [2, 1024, 1024], P('pipe', 'dp')
- g_keyval: float32 [2, 1024, 1024], P('pipe', 'dp')
- g_out: float32 [2, 1024, 1024], P('pipe', 'dp')
- g_norm_ffn: float32 [2, 1024], P('pipe', 'dp')
- g_router: float32 [2, 1024, 32], P('pipe', 'dp')
- g_gate: float32 [2, 32, 1024, 512], P('pipe', 'expert', None, 'dp')
- g_up: float32 [2, 32, 1024, 512], P('pipe', 'expert', None, 'dp')
- g_down: float32 [2, 32, 512, 1024], P('pipe', 'expert', 'dp')
Inputs may be any that keep to these rules, and one draw needn't show every extreme that they name: `routes`: within every block of 64 rows (the tokens of one sequence of one layer) no expert is named by more than 20 rows, a bound that some block reaches; a row names 8 different experts. `segments`: along every sequence segment numbers never fall; each segment holds 1 to 32 positions and one holds exactly 32.
All inputs are finite; a program needn't handle non-finite values.
Results may differ from a plain program's by a relative error of at most 0.028.
Values may be sent and summed in bfloat16 or wider, within the bound.
A program may use at most 256 MiB of HBM per device.

v0:
```python
import jax
import jax.numpy as jnp
from jax import lax
from jax.sharding import PartitionSpec as P

QUERY_HEADS = 16
KEY_VALUE_HEADS = 8
HEAD_DIMENSION = 64
EXPERTS = 32
TOP = 8
CAP = 20


epsilon = 1e-06
rope_base = 10000.0
highest = lax.Precision.HIGHEST


def shifted(block, axis, distance):
    devices = range(lax.axis_size(axis))
    route = [(i - distance, i) for i in devices if i - distance in devices]
    return lax.ppermute(block, axis, route)


def normed(values_in, gain_vec):
    return (
        values_in
        * lax.rsqrt(jnp.mean(values_in * values_in, axis=-1, keepdims=True) + epsilon)
        * gain_vec
    )


def rotary_embed(values_in, token_position):
    half_dim = values_in.shape[-1] // 2
    frequency = rope_base ** (-jnp.arange(half_dim, dtype=jnp.float32) / half_dim)
    angles = token_position.astype(jnp.float32)[..., None, None] * frequency
    cosine = jnp.cos(angles)
    sine_part = jnp.sin(angles)
    leading = values_in[..., :half_dim]
    trailing = values_in[..., half_dim:]
    return jnp.concatenate(
        [leading * cosine - trailing * sine_part, trailing * cosine + leading * sine_part], axis=-1
    )


def positions(segment):
    earlier = jnp.sum((segment[..., None, :] < segment[..., :, None]).astype(jnp.int32), axis=-1)
    return jnp.arange(segment.shape[-1], dtype=jnp.int32) - earlier


def causal(segment):
    order_idx = jnp.arange(segment.shape[-1], dtype=jnp.int32)
    return (segment[..., :, None] == segment[..., None, :]) & (
        order_idx[None, :] <= order_idx[:, None]
    )


def places(routing):
    flat_ids = routing.reshape(routing.shape[:-2] + (-1,))
    onehot = (flat_ids[..., None] == jnp.arange(EXPERTS, dtype=jnp.int32)).astype(jnp.int32)
    earlier_count = jnp.cumsum(onehot, axis=-2) - onehot
    return flat_ids * CAP + jnp.sum(earlier_count * onehot, axis=-1)


def attention_scores(query_matrix, key_matrix, allowed):
    sequence_length = query_matrix.shape[0]
    grouped_queries = query_matrix.reshape(
        sequence_length, KEY_VALUE_HEADS, QUERY_HEADS // KEY_VALUE_HEADS, HEAD_DIMENSION
    )
    scores = jnp.einsum(
        "qhgd,khd->hgqk", grouped_queries, key_matrix, preferred_element_type=jnp.float32
    ) * HEAD_DIMENSION ** (-0.5)
    return jnp.where(allowed[None, None], scores, -1e30)


def fetch_weights(w_query, key_value_weight, w_out):
    return (
        lax.all_gather(w_query[0], "dp", axis=0, tiled=True),
        lax.all_gather(key_value_weight[0], "dp", axis=0, tiled=True),
        lax.all_gather(w_out[0], "dp", axis=0, tiled=True),
    )


def store_micro(buffer, micro_idx, active, new_value):
    previous = lax.dynamic_index_in_dim(buffer, micro_idx, 0, keepdims=False)
    return lax.dynamic_update_index_in_dim(
        buffer, jnp.where(active, new_value, previous), micro_idx, 0
    )


def forward_layer(
    stream, segment, routing, gathered, gain_attn, gain_ffn, router, gate_w, up_w, down_w
):
    full_query, full_keyval, full_out = gathered
    sequence_length, model_width = stream.shape
    attn_normed = normed(stream, gain_attn).astype(jnp.bfloat16)
    query_lin = jnp.dot(attn_normed, full_query, preferred_element_type=jnp.float32)
    key_value_linear = jnp.dot(attn_normed, full_keyval, preferred_element_type=jnp.float32)
    token_position = positions(segment)
    split_index = KEY_VALUE_HEADS * HEAD_DIMENSION
    query_matrix = rotary_embed(
        query_lin.reshape(sequence_length, QUERY_HEADS, HEAD_DIMENSION), token_position
    ).astype(jnp.bfloat16)
    key_matrix = rotary_embed(
        key_value_linear[:, :split_index].reshape(sequence_length, KEY_VALUE_HEADS, HEAD_DIMENSION),
        token_position,
    ).astype(jnp.bfloat16)
    value_matrix = (
        key_value_linear[:, split_index:]
        .reshape(sequence_length, KEY_VALUE_HEADS, HEAD_DIMENSION)
        .astype(jnp.bfloat16)
    )
    scores = attention_scores(query_matrix, key_matrix, causal(segment))
    row_peak = jnp.max(scores, axis=-1, keepdims=True)
    exponent = jnp.exp(scores - row_peak)
    totals = jnp.sum(exponent, axis=-1, keepdims=True)
    attend_weights = (exponent / totals).astype(jnp.bfloat16)
    log_total = row_peak + jnp.log(totals)
    attended = jnp.einsum(
        "hgqk,khd->qhgd", attend_weights, value_matrix, preferred_element_type=jnp.float32
    )
    attended = attended.reshape(sequence_length, QUERY_HEADS * HEAD_DIMENSION).astype(jnp.bfloat16)
    middle = stream + jnp.dot(attended, full_out, preferred_element_type=jnp.float32)
    ffn_normed = normed(middle, gain_ffn).astype(jnp.bfloat16)
    logits = jnp.dot(ffn_normed, router, preferred_element_type=jnp.float32)
    gates = jax.nn.softmax(jnp.take_along_axis(logits, routing, axis=1), axis=-1)
    slot_place = places(routing)
    slot_table = (
        jnp.full((EXPERTS * CAP,), sequence_length, jnp.int32)
        .at[slot_place]
        .set(jnp.arange(sequence_length * TOP, dtype=jnp.int32) // TOP)
    )
    padded = jnp.concatenate([ffn_normed, jnp.zeros((1, model_width), jnp.bfloat16)], axis=0)
    outgoing = padded[slot_table].reshape(EXPERTS, 1, CAP, model_width)
    slot_rows = lax.all_to_all(outgoing, "expert", split_axis=0, concat_axis=1, tiled=True)
    gate_lin = jnp.einsum("encd,edf->encf", slot_rows, gate_w, preferred_element_type=jnp.float32)
    up_lin = jnp.einsum("encd,edf->encf", slot_rows, up_w, preferred_element_type=jnp.float32)
    inner_act = (jax.nn.silu(gate_lin) * up_lin).astype(jnp.bfloat16)
    produced = jnp.einsum(
        "encf,efd->encd", inner_act, down_w, preferred_element_type=jnp.float32
    ).astype(jnp.bfloat16)
    produced, gate_lin, up_lin, slot_rows = (produced, gate_lin, up_lin, slot_rows)
    returned = lax.all_to_all(produced, "expert", split_axis=1, concat_axis=0, tiled=True).reshape(
        EXPERTS * CAP, model_width
    )
    picked = returned[slot_place].reshape(sequence_length, TOP, model_width)
    mixture_out = jnp.einsum("sk,skd->sd", gates, picked.astype(jnp.float32), precision=highest)
    retained = (
        stream,
        attn_normed,
        query_matrix,
        key_matrix,
        value_matrix,
        log_total,
        attended,
        middle,
        ffn_normed,
        gates,
        slot_place,
        picked,
        gate_lin,
        up_lin,
        slot_rows,
    )
    return (middle + mixture_out, retained)


def backward_layer(
    carried, retained, segment, routing, gathered, gain_attn, gain_ffn, router, gate_w, up_w, down_w
):
    full_query, full_keyval, full_out = gathered
    (
        stream,
        attn_normed,
        query_matrix,
        key_matrix,
        value_matrix,
        log_total,
        attended,
        middle,
        ffn_normed,
        gates,
        slot_place,
        picked,
        gate_lin,
        up_lin,
        slot_rows,
    ) = retained
    sequence_length, model_width = carried.shape
    gate_grad = jnp.einsum("sd,skd->sk", carried, picked.astype(jnp.float32), precision=highest)
    chosen_grad = gates * (gate_grad - jnp.sum(gates * gate_grad, axis=-1, keepdims=True))
    choose = (routing[:, :, None] == jnp.arange(EXPERTS, dtype=jnp.int32)).astype(jnp.float32)
    logit_grad = jnp.sum(choose * chosen_grad[:, :, None], axis=1)
    router_grad = jnp.einsum(
        "sd,se->de", ffn_normed.astype(jnp.float32), logit_grad, precision=highest
    )
    ffn_grad = jnp.einsum("se,de->sd", logit_grad, router.astype(jnp.float32), precision=highest)
    product_grad = (
        (gates[:, :, None] * carried[:, None, :])
        .astype(jnp.bfloat16)
        .reshape(sequence_length * TOP, model_width)
    )
    outgoing = (
        jnp.zeros((EXPERTS * CAP, model_width), jnp.bfloat16).at[slot_place].set(product_grad)
    )
    outgoing = outgoing.reshape(EXPERTS, 1, CAP, model_width)
    arriving = lax.all_to_all(outgoing, "expert", split_axis=0, concat_axis=1, tiled=True)
    inner_act, inner_pull = jax.vjp(
        lambda gate_in, up_in: jax.nn.silu(gate_in) * up_in, gate_lin, up_lin
    )
    inner_grad = jnp.einsum("encd,efd->encf", arriving, down_w, preferred_element_type=jnp.float32)
    gate_grad_lin, up_grad_lin = inner_pull(inner_grad)
    gate_low = gate_grad_lin.astype(jnp.bfloat16)
    up_low = up_grad_lin.astype(jnp.bfloat16)
    rows_grad = jnp.einsum("encf,edf->encd", gate_low, gate_w, preferred_element_type=jnp.float32)
    rows_grad = (
        rows_grad + jnp.einsum("encf,edf->encd", up_low, up_w, preferred_element_type=jnp.float32)
    ).astype(jnp.bfloat16)
    sent_back = lax.all_to_all(
        rows_grad, "expert", split_axis=1, concat_axis=0, tiled=True
    ).reshape(EXPERTS * CAP, model_width)
    ffn_grad = ffn_grad + jnp.sum(
        sent_back[slot_place].reshape(sequence_length, TOP, model_width).astype(jnp.float32), axis=1
    )
    middle_grad, gain_ffn_grad = jax.vjp(normed, middle, gain_ffn)[1](ffn_grad)
    middle_grad = middle_grad + carried
    branch_grad = middle_grad.astype(jnp.bfloat16)
    attention_output_grad = jnp.einsum(
        "sd,ed->se", branch_grad, full_out, preferred_element_type=jnp.float32
    ).astype(jnp.bfloat16)
    query_group_size = QUERY_HEADS // KEY_VALUE_HEADS
    grouped_gradient = attention_output_grad.reshape(
        sequence_length, KEY_VALUE_HEADS, query_group_size, HEAD_DIMENSION
    )
    scores = attention_scores(query_matrix, key_matrix, causal(segment))
    attend_prob = jnp.exp(scores - log_total)
    prob_grad = jnp.einsum(
        "qhgd,khd->hgqk", grouped_gradient, value_matrix, preferred_element_type=jnp.float32
    )
    score_grad = (
        attend_prob * (prob_grad - jnp.sum(prob_grad * attend_prob, axis=-1, keepdims=True))
    ).astype(jnp.bfloat16)
    grouped_queries = query_matrix.reshape(
        sequence_length, KEY_VALUE_HEADS, query_group_size, HEAD_DIMENSION
    )
    query_grad = jnp.einsum(
        "hgqk,khd->qhgd", score_grad, key_matrix, preferred_element_type=jnp.float32
    ).reshape(sequence_length, QUERY_HEADS, HEAD_DIMENSION) * HEAD_DIMENSION ** (-0.5)
    key_gradient = jnp.einsum(
        "hgqk,qhgd->khd", score_grad, grouped_queries, preferred_element_type=jnp.float32
    ) * HEAD_DIMENSION ** (-0.5)
    value_gradient = jnp.einsum(
        "hgqk,qhgd->khd",
        attend_prob.astype(jnp.bfloat16),
        grouped_gradient,
        preferred_element_type=jnp.float32,
    )
    token_position = positions(segment)
    query_back = jax.vjp(
        lambda rotated_rows: rotary_embed(rotated_rows, token_position),
        jnp.zeros((sequence_length, QUERY_HEADS, HEAD_DIMENSION), jnp.float32),
    )[1]
    key_pullback = jax.vjp(
        lambda rotated_rows: rotary_embed(rotated_rows, token_position),
        jnp.zeros((sequence_length, KEY_VALUE_HEADS, HEAD_DIMENSION), jnp.float32),
    )[1]
    query_low = (
        query_back(query_grad)[0]
        .reshape(sequence_length, QUERY_HEADS * HEAD_DIMENSION)
        .astype(jnp.bfloat16)
    )
    keyval_low = jnp.concatenate(
        [
            key_pullback(key_gradient)[0].reshape(
                sequence_length, KEY_VALUE_HEADS * HEAD_DIMENSION
            ),
            value_gradient.reshape(sequence_length, KEY_VALUE_HEADS * HEAD_DIMENSION),
        ],
        axis=1,
    ).astype(jnp.bfloat16)
    normed_grad = jnp.einsum("se,de->sd", query_low, full_query, preferred_element_type=jnp.float32)
    normed_grad = normed_grad + jnp.einsum(
        "se,de->sd", keyval_low, full_keyval, preferred_element_type=jnp.float32
    )
    stream_grad, gain_attn_grad = jax.vjp(normed, stream, gain_attn)[1](normed_grad)
    small_grads = (gain_attn_grad, gain_ffn_grad, router_grad)
    operands = (
        query_low,
        keyval_low,
        branch_grad,
        gate_low,
        up_low,
        inner_act.astype(jnp.bfloat16),
        arriving,
    )
    return (stream_grad + middle_grad, small_grads, operands)


def on_device(
    inputs,
    cotangent,
    segments,
    routes,
    norm_attn,
    w_query,
    key_value_weight,
    w_out,
    norm_ffn,
    w_router,
    w_gate,
    w_up,
    w_down,
):
    sections = lax.axis_size("pipe")
    section_idx = lax.axis_index("pipe")
    micro_batches = inputs.shape[0]
    sequence_length, model_width = (inputs.shape[2], inputs.shape[3])
    tick_count = micro_batches + sections - 1
    layer_params = (norm_attn[0], norm_ffn[0], w_router[0], w_gate[0], w_up[0], w_down[0])
    hidden = jnp.zeros((micro_batches, sequence_length, model_width), jnp.float32)
    arrived = jnp.zeros((sequence_length, model_width), jnp.float32)
    stashed = None
    for step_idx in range(tick_count):
        offset = step_idx - section_idx
        micro_idx = jnp.clip(offset, 0, micro_batches - 1)
        active = (offset >= 0) & (offset < micro_batches)
        gathered = fetch_weights(w_query, key_value_weight, w_out)
        own_rows = lax.dynamic_index_in_dim(inputs, micro_idx, 0, keepdims=False)[0].astype(
            jnp.float32
        )
        stream = jnp.where(section_idx == 0, own_rows, arrived)
        segment = lax.dynamic_index_in_dim(segments, micro_idx, 0, keepdims=False)[0]
        routing = lax.dynamic_index_in_dim(routes[0], micro_idx, 0, keepdims=False)[0]
        result, retained = forward_layer(stream, segment, routing, gathered, *layer_params)
        if stashed is None:
            stashed = jax.tree.map(
                lambda leaf_arr: jnp.zeros((micro_batches,) + leaf_arr.shape, leaf_arr.dtype),
                retained,
            )
        stashed = jax.tree.map(
            lambda buffer, leaf_arr: store_micro(buffer, micro_idx, active, leaf_arr),
            stashed,
            retained,
        )
        hidden = store_micro(hidden, micro_idx, active, result)
        if step_idx < tick_count - 1:
            arrived = shifted(result.astype(jnp.bfloat16), "pipe", 1).astype(result.dtype)
    grad_in = jnp.zeros_like(hidden)
    returned = jnp.zeros((sequence_length, model_width), jnp.float32)
    small_totals = None
    kept_operands = None
    for step_idx in range(tick_count):
        offset = step_idx - (sections - 1 - section_idx)
        micro_idx = jnp.clip(offset, 0, micro_batches - 1)
        active = (offset >= 0) & (offset < micro_batches)
        gathered = fetch_weights(w_query, key_value_weight, w_out)
        own_cot = lax.dynamic_index_in_dim(cotangent, micro_idx, 0, keepdims=False)[0].astype(
            jnp.float32
        )
        carried = jnp.where(section_idx == sections - 1, own_cot, returned)
        segment = lax.dynamic_index_in_dim(segments, micro_idx, 0, keepdims=False)[0]
        routing = lax.dynamic_index_in_dim(routes[0], micro_idx, 0, keepdims=False)[0]
        retained = jax.tree.map(
            lambda buffer: lax.dynamic_index_in_dim(buffer, micro_idx, 0, keepdims=False), stashed
        )
        stream_grad, small_grads, operands = backward_layer(
            carried, retained, segment, routing, gathered, *layer_params
        )
        masked = jax.tree.map(lambda leaf_arr: jnp.where(active, leaf_arr, 0.0), small_grads)
        small_totals = (
            masked if small_totals is None else jax.tree.map(jnp.add, small_totals, masked)
        )
        if kept_operands is None:
            kept_operands = jax.tree.map(
                lambda leaf_arr: jnp.zeros((micro_batches,) + leaf_arr.shape, leaf_arr.dtype),
                operands,
            )
        kept_operands = jax.tree.map(
            lambda buffer, leaf_arr: store_micro(buffer, micro_idx, active, leaf_arr),
            kept_operands,
            operands,
        )
        grad_in = store_micro(grad_in, micro_idx, active, stream_grad)
        if step_idx < tick_count - 1:
            returned = shifted(stream_grad.astype(jnp.bfloat16), "pipe", -1).astype(
                stream_grad.dtype
            )
    attn_gain_grad, ffn_gain_grad, router_grad = small_totals
    query_lows, keyval_lows, branch_grads, gate_lows, up_lows, inner_lows, arrivals = kept_operands
    kept_normed = stashed[1]
    kept_attended = stashed[6]
    kept_slots = stashed[14]
    query_grad = jnp.einsum(
        "msd,mse->de", kept_normed, query_lows, preferred_element_type=jnp.float32
    )
    keyval_grad = jnp.einsum(
        "msd,mse->de", kept_normed, keyval_lows, preferred_element_type=jnp.float32
    )
    out_grad = jnp.einsum(
        "mse,msd->ed", kept_attended, branch_grads, preferred_element_type=jnp.float32
    )
    gate_grad = jnp.einsum(
        "mencd,mencf->edf", kept_slots, gate_lows, preferred_element_type=jnp.float32
    )
    up_grad = jnp.einsum(
        "mencd,mencf->edf", kept_slots, up_lows, preferred_element_type=jnp.float32
    )
    down_grad = jnp.einsum(
        "mencf,mencd->efd", inner_lows, arrivals, preferred_element_type=jnp.float32
    )
    part_gain_a, part_query, part_keyval, part_out, part_gain_f, part_router = (
        lax.psum_scatter(
            attn_gain_grad[None].astype(jnp.bfloat16), "dp", scatter_dimension=1, tiled=True
        ).astype(jnp.float32),
        lax.psum_scatter(
            query_grad[None].astype(jnp.bfloat16), "dp", scatter_dimension=1, tiled=True
        ).astype(jnp.float32),
        lax.psum_scatter(
            keyval_grad[None].astype(jnp.bfloat16), "dp", scatter_dimension=1, tiled=True
        ).astype(jnp.float32),
        lax.psum_scatter(
            out_grad[None].astype(jnp.bfloat16), "dp", scatter_dimension=1, tiled=True
        ).astype(jnp.float32),
        lax.psum_scatter(
            ffn_gain_grad[None].astype(jnp.bfloat16), "dp", scatter_dimension=1, tiled=True
        ).astype(jnp.float32),
        lax.psum_scatter(
            router_grad[None].astype(jnp.bfloat16), "dp", scatter_dimension=1, tiled=True
        ).astype(jnp.float32),
    )
    sum_gain_a, sum_query, sum_keyval, sum_out, sum_gain_f, sum_router = (
        lax.psum(part_gain_a.astype(jnp.bfloat16), "expert").astype(jnp.float32),
        lax.psum(part_query.astype(jnp.bfloat16), "expert").astype(jnp.float32),
        lax.psum(part_keyval.astype(jnp.bfloat16), "expert").astype(jnp.float32),
        lax.psum(part_out.astype(jnp.bfloat16), "expert").astype(jnp.float32),
        lax.psum(part_gain_f.astype(jnp.bfloat16), "expert").astype(jnp.float32),
        lax.psum(part_router.astype(jnp.bfloat16), "expert").astype(jnp.float32),
    )
    sum_gate, sum_up, sum_down = (
        lax.psum_scatter(
            gate_grad[None].astype(jnp.bfloat16), "dp", scatter_dimension=3, tiled=True
        ).astype(jnp.float32),
        lax.psum_scatter(
            up_grad[None].astype(jnp.bfloat16), "dp", scatter_dimension=3, tiled=True
        ).astype(jnp.float32),
        lax.psum_scatter(
            down_grad[None].astype(jnp.bfloat16), "dp", scatter_dimension=2, tiled=True
        ).astype(jnp.float32),
    )
    return (
        hidden[None, :, None],
        grad_in[None, :, None],
        sum_gain_a,
        sum_query,
        sum_keyval,
        sum_out,
        sum_gain_f,
        sum_router,
        sum_gate,
        sum_up,
        sum_down,
    )


def solution(mesh):
    return jax.shard_map(
        on_device,
        mesh=mesh,
        in_specs=(
            P(None, ("dp", "expert"), None, None),
            P(None, ("dp", "expert"), None, None),
            P(None, ("dp", "expert"), None),
            P("pipe", None, ("dp", "expert"), None, None),
            P("pipe", None),
            P("pipe", "dp", None),
            P("pipe", "dp", None),
            P("pipe", "dp", None),
            P("pipe", None),
            P("pipe", None, None),
            P("pipe", "expert", None, None),
            P("pipe", "expert", None, None),
            P("pipe", "expert", None, None),
        ),
        out_specs=(
            P("pipe", None, ("dp", "expert"), None, None),
            P("pipe", None, ("dp", "expert"), None, None),
            P("pipe", "dp"),
            P("pipe", "dp", None),
            P("pipe", "dp", None),
            P("pipe", "dp", None),
            P("pipe", "dp"),
            P("pipe", "dp", None),
            P("pipe", "expert", None, "dp"),
            P("pipe", "expert", None, "dp"),
            P("pipe", "expert", "dp", None),
        ),
        check_vma=False,
    )
```

profile of v0, /device:TPU:0, one launch (start us, length us, event | category | flops | bytes accessed | tf_op | source)
XLA Modules:
  0.0 1444.6 jit_solution(4561823841114088736)
XLA Ops:
  16.5 31.4 %all-gather.7.cloned.1.call-done = bf16[1,1024,1024]{2,1,0:T(8,128)(2,1)} async-done(((bf16[1,256,1024]{2,1,0:T(8,128)(2,1)}), bf16[1,1024,1024]{2,1,0:T(8,128)(2,1)}) %all-gather.7.cloned.1.call-update) | async-done | bytes 2097168 | tf_op jit(solution)/shard_map/all_gather | solution.py:79
  50.9 34.2 %all-gather.9.cloned.1.call-done = bf16[1,1024,1024]{2,1,0:T(8,128)(2,1)} async-done(((bf16[1,256,1024]{2,1,0:T(8,128)(2,1)}), bf16[1,1024,1024]{2,1,0:T(8,128)(2,1)}) %all-gather.9.cloned.1.call-update) | async-done | bytes 2097168 | tf_op jit(solution)/shard_map/all_gather | solution.py:78
  91.7 30.6 %all-gather.11.cloned.1.call-done = bf16[1,1024,1024]{2,1,0:T(8,128)(2,1)} async-done(((bf16[1,256,1024]{2,1,0:T(8,128)(2,1)}), bf16[1,1024,1024]{2,1,0:T(8,128)(2,1)}) %all-gather.11.cloned.1.call-update) | async-done | bytes 2097168 | tf_op jit(solution)/shard_map/all_gather | solution.py:80
  130.2 4.8 all-to-all-start
  137.9 34.0 %all-to-all-done = bf16[32,1,20,1024]{3,2,1,0:T(8,128)(2,1)S(1)} async-done(((bf16[32,1,20,1024]{3,2,1,0:T(8,128)(2,1)}), bf16[32,1,20,1024]{3,2,1,0:T(8,128)(2,1)S(1)}, u32[]{:S(2)}, u32[]{:S(2)}) %all-to-all-start) | async-done | bytes 1310752 | tf_op jit(solution)/shard_map/all_to_all | solution.py:135
  172.3 5.8 bitcast_dynamic-update-slice_fusion.7
  187.4 3.5 all-to-all-start.1
  198.8 3.9 gather_fusion.9
  203.9 17.9 %all-to-all-done.1 = bf16[8,4,20,1024]{3,0,2,1:T(8,128)(2,1)S(1)} async-done(((bf16[8,4,20,1024]{3,0,2,1:T(8,128)(2,1)}), bf16[8,4,20,1024]{3,0,2,1:T(8,128)(2,1)S(1)}, u32[]{:S(2)}, u32[]{:S(2)}) %all-to-all-start.1) | async-done | bytes 1310752 | tf_op jit(solution)/shard_map/all_to_all | solution.py:143
  260.2 4.5 all-to-all-start.2
  274.5 26.1 %all-to-all-done.2 = bf16[32,1,20,1024]{3,2,1,0:T(8,128)(2,1)} async-done(((bf16[32,1,20,1024]{3,2,1,0:T(8,128)(2,1)}), bf16[32,1,20,1024]{3,2,1,0:T(8,128)(2,1)}, u32[]{:S(2)}, u32[]{:S(2)}) %all-to-all-start.2) | async-done | bytes 1310752 | tf_op jit(solution)/shard_map/all_to_all | solution.py:135
  300.6 7.1 bitcast_dynamic-update-slice_fusion.6
  307.8 6.8 bitcast_dynamic-update-slice_fusion.3
  317.9 3.7 all-to-all-start.3
  329.9 3.9 gather_fusion.10
  337.9 14.5 %all-to-all-done.3 = bf16[8,4,20,1024]{3,0,2,1:T(8,128)(2,1)S(1)} async-done(((bf16[8,4,20,1024]{3,0,2,1:T(8,128)(2,1)}), bf16[8,4,20,1024]{3,0,2,1:T(8,128)(2,1)S(1)}, u32[]{:S(2)}, u32[]{:S(2)}) %all-to-all-start.3) | async-done | bytes 1310752 | tf_op jit(solution)/shard_map/all_to_all | solution.py:143
  386.5 4.4 all-to-all-start.4
  407.2 20.8 %all-to-all-done.4 = bf16[32,1,20,1024]{3,2,1,0:T(8,128)(2,1)} async-done(((bf16[32,1,20,1024]{3,2,1,0:T(8,128)(2,1)}), bf16[32,1,20,1024]{3,2,1,0:T(8,128)(2,1)}, u32[]{:S(2)}, u32[]{:S(2)}) %all-to-all-start.4) | async-done | bytes 1310752 | tf_op jit(solution)/shard_map/all_to_all | solution.py:135
  428.1 7.1 bitcast_dynamic-update-slice_fusion.5
  435.2 6.8 bitcast_dynamic-update-slice_fusion.2
  445.4 4.6 all-to-all-start.5
  457.3 3.9 gather_fusion.11
  462.4 18.6 %all-to-all-done.5 = bf16[8,4,20,1024]{3,0,2,1:T(8,128)(2,1)} async-done(((bf16[8,4,20,1024]{3,0,2,1:T(8,128)(2,1)}), bf16[8,4,20,1024]{3,0,2,1:T(8,128)(2,1)}, u32[]{:S(2)}, u32[]{:S(2)}) %all-to-all-start.5) | async-done | bytes 1310752 | tf_op jit(solution)/shard_map/all_to_all | solution.py:143
  501.5 4.7 all-to-all-start.6
  523.6 19.2 %all-to-all-done.6 = bf16[32,1,20,1024]{3,2,1,0:T(8,128)(2,1)} async-done(((bf16[32,1,20,1024]{3,2,1,0:T(8,128)(2,1)}), bf16[32,1,20,1024]{3,2,1,0:T(8,128)(2,1)}, u32[]{:S(2)}, u32[]{:S(2)}) %all-to-all-start.6) | async-done | bytes 1310752 | tf_op jit(solution)/shard_map/all_to_all | solution.py:207
  542.9 7.2 bitcast_dynamic-update-slice_fusion.11
  551.3 6.2 fusion.16
  557.7 4.6 bitcast_dynamic-update-slice_fusion.14
  568.0 4.8 all-to-all-start.7
  580.3 23.3 %all-to-all-done.7 = bf16[8,4,20,1024]{3,0,2,1:T(8,128)(2,1)} async-done(((bf16[8,4,20,1024]{3,0,2,1:T(8,128)(2,1)}), bf16[8,4,20,1024]{3,0,2,1:T(8,128)(2,1)}, u32[]{:S(2)}, u32[]{:S(2)}) %all-to-all-start.7) | async-done | bytes 1310752 | tf_op jit(solution)/shard_map/all_to_all | solution.py:219
  631.5 3.8 scatter_custom_fusion.4
  638.5 4.5 all-to-all-start.8
  646.2 34.4 %all-to-all-done.8 = bf16[32,1,20,1024]{3,2,1,0:T(8,128)(2,1)} async-done(((bf16[32,1,20,1024]{3,2,1,0:T(8,128)(2,1)}), bf16[32,1,20,1024]{3,2,1,0:T(8,128)(2,1)}, u32[]{:S(2)}, u32[]{:S(2)}) %all-to-all-start.8) | async-done | bytes 1310752 | tf_op jit(solution)/shard_map/all_to_all | solution.py:207
  680.6 11.0 bitcast_dynamic-update-slice_fusion.13
  691.6 6.0 fusion.14
  697.7 6.1 add_convert_fusion.1
  705.6 4.6 all-to-all-start.9
  712.1 29.2 %all-to-all-done.9 = bf16[8,4,20,1024]{3,0,2,1:T(8,128)(2,1)} async-done(((bf16[8,4,20,1024]{3,0,2,1:T(8,128)(2,1)}), bf16[8,4,20,1024]{3,0,2,1:T(8,128)(2,1)}, u32[]{:S(2)}, u32[]{:S(2)}) %all-to-all-start.9) | async-done | bytes 1310752 | tf_op jit(solution)/shard_map/all_to_all | solution.py:219
  769.3 3.7 scatter_custom_fusion.5
  776.3 4.7 all-to-all-start.10
  784.2 34.5 %all-to-all-done.10 = bf16[32,1,20,1024]{3,2,1,0:T(8,128)(2,1)} async-done(((bf16[32,1,20,1024]{3,2,1,0:T(8,128)(2,1)}), bf16[32,1,20,1024]{3,2,1,0:T(8,128)(2,1)}, u32[]{:S(2)}, u32[]{:S(2)}) %all-to-all-start.10) | async-done | bytes 1310752 | tf_op jit(solution)/shard_map/all_to_all | solution.py:207
  818.6 9.4 bitcast_dynamic-update-slice_fusion.12
  828.1 6.0 fusion.12
  834.1 6.1 add_convert_fusion
  842.0 4.4 all-to-all-start.11
  848.9 28.7 %all-to-all-done.11 = bf16[8,4,20,1024]{3,0,2,1:T(8,128)(2,1)} async-done(((bf16[8,4,20,1024]{3,0,2,1:T(8,128)(2,1)}), bf16[8,4,20,1024]{3,0,2,1:T(8,128)(2,1)}, u32[]{:S(2)}, u32[]{:S(2)}) %all-to-all-start.11) | async-done | bytes 1310752 | tf_op jit(solution)/shard_map/all_to_all | solution.py:219
  935.9 3.7 fusion.105
  939.6 34.0 %reduce-scatter.20.cloned.1.call-done = bf16[1,256,1024]{2,1,0:T(8,128)(2,1)} async-done(((bf16[1,1024,1024]{2,1,0:T(8,128)(2,1)}), bf16[1,256,1024]{2,1,0:T(8,128)(2,1)}) %reduce-scatter.20.cloned.1.call-update) | async-done | bytes 524304 | tf_op jit(solution)/shard_map/reduce_scatter | solution.py:418
  973.6 38.0 %reduce-scatter.22.cloned.1.call-done = bf16[1,256,1024]{2,1,0:T(8,128)(2,1)} async-done(((bf16[1,1024,1024]{2,1,0:T(8,128)(2,1)}), bf16[1,256,1024]{2,1,0:T(8,128)(2,1)}) %reduce-scatter.22.cloned.1.call-update) | async-done | bytes 524304 | tf_op jit(solution)/shard_map/reduce_scatter | solution.py:421
  1011.7 7.8 fusion.36
  1019.5 12.5 copy.595
  1032.0 16.5 %copy.613 = bf16[64,8,8,1024]{3,1,2,0:T(8,128)(2,1)} copy(bf16[64,8,8,1024]{3,2,1,0:T(8,128)(2,1)} %bitcast.1402) | data formatting | bytes 16777216
  1050.0 7.7 fusion.37
  1057.7 12.6 copy.597
  1070.2 16.5 %copy.615 = bf16[64,8,8,1024]{3,1,2,0:T(8,128)(2,1)} copy(bf16[64,8,8,1024]{3,2,1,0:T(8,128)(2,1)} %bitcast.1403) | data formatting | bytes 16777216
  1093.7 7.3 fusion.38
  1106.8 20.8 %all-reduce.15 = (bf16[1,256]{1,0:T(2,128)(2,1)S(1)}, bf16[1,256]{1,0:T(2,128)(2,1)S(1)}, bf16[1,256,32]{1,2,0:T(8,128)(2,1)S(1)}) all-reduce(bf16[1,256]{1,0:T(2,128)(2,1)S(1)} %copy.592, bf16[1,256]{1,0:T(2,128)(2,1)S(1)} %copy.594, ...), channel_id=1, replica_groups=mesh['pipe'=2,'dp'=4,'expert'=4] {'expert'}, use_global_device_ids=true, to_apply=%region_67.69 | all-reduce | flops 8704 | bytes 34816 | tf_op jit(solution)/shard_map/psum | solution.py:432
  1129.3 36.9 %all-reduce.19.cloned.1.call-done = (bf16[1,256,1024]{2,1,0:T(8,128)(2,1)}, bf16[1,256,1024]{2,1,0:T(8,128)(2,1)}, bf16[1,256,1024]{2,1,0:T(8,128)(2,1)}) async-done(((bf16[1,256,1024]{2,1,0:T(8,128)(2,1)}, bf16[1,256,1024]{2,1,0:T(8,128)(2,1)}, bf16[1,256,1024]{2,1,0:T(8,128)(2,1)}), (bf16[1,256,1024]{2,1,0:T(8,128)(2,1)}, bf16[1,256,1024]{2,1,0:T(8,128)(2,1)}, ...) | async-done | bytes 1572880 | tf_op jit(solution)/shard_map/psum | solution.py:433
  1170.6 84.1 %reduce-scatter.32.cloned.1.call-done = bf16[128,8192]{1,0:T(8,128)(2,1)} async-done(((bf16[512,8192]{1,0:T(8,128)(2,1)}), bf16[128,8192]{1,0:T(8,128)(2,1)}) %reduce-scatter.32.cloned.1.call-update) | async-done | bytes 2097168
  1254.7 4.3 copy.614
  1264.6 79.8 %reduce-scatter.34.cloned.1.call-done = bf16[128,8192]{1,0:T(8,128)(2,1)} async-done(((bf16[512,8192]{1,0:T(8,128)(2,1)}), bf16[128,8192]{1,0:T(8,128)(2,1)}) %reduce-scatter.34.cloned.1.call-update) | async-done | bytes 2097168
  1344.3 4.3 copy.616
  1354.3 79.5 %reduce-scatter.26.cloned.1.call-done = bf16[1,8,128,1024]{3,2,1,0:T(8,128)(2,1)} async-done(((bf16[1,8,512,1024]{3,2,1,0:T(8,128)(2,1)}), bf16[1,8,128,1024]{3,2,1,0:T(8,128)(2,1)}) %reduce-scatter.26.cloned.1.call-update) | async-done | bytes 2097168 | tf_op jit(solution)/shard_map/reduce_scatter | solution.py:446
  1433.8 4.1 convert_element_type.813
  (993 shorter events, 389.6 us)
Async XLA Ops:
  7.2 191.5 %copy-start = (bf16[1,1024,32]{1,2,0:T(8,128)(2,1)S(1)}, bf16[1,1024,32]{1,2,0:T(8,128)(2,1)}, u32[]{:S(2)}) copy-start(bf16[1,1024,32]{1,2,0:T(8,128)(2,1)} %param.24) | copy-start | bytes 196612
  7.2 9.1 copy-start.26
  7.2 40.7 %copy-start.147 = (f32[1,1024]{1,0:T(1,128)S(1)}, f32[1,1024]{1,0:T(1,128)}, u32[]{:S(2)}) copy-start(f32[1,1024]{1,0:T(1,128)} %param.19) | copy-start | bytes 12292
  7.2 40.7 %all-gather.7.cloned.1.call-start = ((), (), s32[]{:S(2)}) async-start(), calls=%async_computation.26 | async-start | bytes 2621440 | tf_op jit(solution)/shard_map/all_gather | solution.py:79
  8.0 77.2 %all-gather.9.cloned.1.call-start = ((), (), s32[]{:S(2)}) async-start(), calls=%async_computation.27 | async-start | bytes 2621440 | tf_op jit(solution)/shard_map/all_gather | solution.py:78
  8.7 113.6 %all-gather.11.cloned.1.call-start = ((), (), s32[]{:S(2)}) async-start(), calls=%async_computation.28 | async-start | bytes 2621440 | tf_op jit(solution)/shard_map/all_gather | solution.py:80
  10.4 181.5 %copy-start.235 = (s32[512]{0:T(512)}, s32[512]{0:T(512)S(1)}, u32[]{:S(2)}) copy-start(s32[512]{0:T(512)S(1)} %add_select_fusion) | copy-start | bytes 6148
  11.9 255.8 %copy-start.165 = (f32[64,32]{0,1:T(8,128)}, f32[64,32]{0,1:T(8,128)S(1)}, u32[]{:S(2)}) copy-start(f32[64,32]{0,1:T(8,128)S(1)} %get-tuple-element.210) | copy-start | bytes 24580
  12.1 35.8 %copy-start.149 = (s32[1,1,1,64,8]{4,3,2,1,0:T(8,128)}, s32[1,1,1,64,8]{4,3,2,1,0:T(8,128)S(1)}, u32[]{:S(2)}) copy-start(s32[1,1,1,64,8]{4,3,2,1,0:T(8,128)S(1)} %copy.389) | copy-start | bytes 6148
  50.1 37.9 %copy-start.133 = (f32[64,1024]{1,0:T(8,128)}, f32[64,1024]{1,0:T(8,128)S(1)}, u32[]{:S(2)}) copy-start(f32[64,1024]{1,0:T(8,128)S(1)} %fusion.74) | copy-start | bytes 786436
  90.7 33.8 %copy-start.192 = (f32[8,2,64]{2,1,0:T(2,128)}, f32[8,2,64]{2,1,0:T(2,128)S(1)}, u32[]{:S(2)}) copy-start(f32[8,2,64]{2,1,0:T(2,128)S(1)} %fusion.233) | copy-start | bytes 12292
  130.2 41.7 %all-to-all-start = ((bf16[32,1,20,1024]{3,2,1,0:T(8,128)(2,1)}), bf16[32,1,20,1024]{3,2,1,0:T(8,128)(2,1)S(1)}, u32[]{:S(2)}, u32[]{:S(2)}) async-start(bf16[32,1,20,1024]{3,2,1,0:T(8,128)(2,1)} %bitcast.1413), calls=%async_computation | async-start | bytes 3145728 | tf_op jit(solution)/shard_map/all_to_all | solution.py:135
  135.1 56.1 %copy-start.91 = (s32[1,1,1,64,8]{4,3,2,1,0:T(8,128)}, s32[1,1,1,64,8]{4,3,2,1,0:T(8,128)S(1)}, u32[]{:S(2)}) copy-start(s32[1,1,1,64,8]{4,3,2,1,0:T(8,128)S(1)} %copy.408) | copy-start | bytes 6148
  171.9 8.3 copy-start.13
  171.9 9.4 slice-start
  172.3 9.0 slice-start.1
  187.4 34.4 %all-to-all-start.1 = ((bf16[8,4,20,1024]{3,0,2,1:T(8,128)(2,1)}), bf16[8,4,20,1024]{3,0,2,1:T(8,128)(2,1)S(1)}, u32[]{:S(2)}, u32[]{:S(2)}) async-start(bf16[8,4,20,1024]{3,0,2,1:T(8,128)(2,1)} %copy.396), calls=%async_computation.1 | async-start | bytes 2621440 | tf_op jit(solution)/shard_map/all_to_all | solution.py:143
  191.8 10.9 copy-start.202
  191.8 129.8 %copy-start.200 = (s32[512]{0:T(512)}, s32[512]{0:T(512)S(1)}, u32[]{:S(2)}) copy-start(s32[512]{0:T(512)S(1)} %get-tuple-element.257) | copy-start | bytes 6148
  228.0 13.6 copy-start.31
  228.0 14.2 copy-start.1
  232.3 6.5 collective-permute-start
  260.2 8.1 copy-start.167
  260.2 40.4 %all-to-all-start.2 = ((bf16[32,1,20,1024]{3,2,1,0:T(8,128)(2,1)}), bf16[32,1,20,1024]{3,2,1,0:T(8,128)(2,1)}, u32[]{:S(2)}, u32[]{:S(2)}) async-start(bf16[32,1,20,1024]{3,2,1,0:T(8,128)(2,1)} %bitcast.1412), calls=%async_computation.2 | async-start | bytes 3145728 | tf_op jit(solution)/shard_map/all_to_all | solution.py:135
  300.6 14.0 slice-start.9
  317.9 8.2 copy-start.229
  317.9 34.5 %all-to-all-start.3 = ((bf16[8,4,20,1024]{3,0,2,1:T(8,128)(2,1)}), bf16[8,4,20,1024]{3,0,2,1:T(8,128)(2,1)S(1)}, u32[]{:S(2)}, u32[]{:S(2)}) async-start(bf16[8,4,20,1024]{3,0,2,1:T(8,128)(2,1)} %copy.416), calls=%async_computation.3 | async-start | bytes 2621440 | tf_op jit(solution)/shard_map/all_to_all | solution.py:143
  362.7 2.9 collective-permute-start.1
  365.6 10.8 copy-start.90
  386.5 41.6 %all-to-all-start.4 = ((bf16[32,1,20,1024]{3,2,1,0:T(8,128)(2,1)}), bf16[32,1,20,1024]{3,2,1,0:T(8,128)(2,1)}, u32[]{:S(2)}, u32[]{:S(2)}) async-start(bf16[32,1,20,1024]{3,2,1,0:T(8,128)(2,1)} %bitcast.1410), calls=%async_computation.4 | async-start | bytes 3145728 | tf_op jit(solution)/shard_map/all_to_all | solution.py:135
  428.1 14.0 slice-start.11
  445.4 35.5 %all-to-all-start.5 = ((bf16[8,4,20,1024]{3,0,2,1:T(8,128)(2,1)}), bf16[8,4,20,1024]{3,0,2,1:T(8,128)(2,1)}, u32[]{:S(2)}, u32[]{:S(2)}) async-start(bf16[8,4,20,1024]{3,0,2,1:T(8,128)(2,1)} %copy.436), calls=%async_computation.5 | async-start | bytes 2621440 | tf_op jit(solution)/shard_map/all_to_all | solution.py:143
  501.5 41.2 %all-to-all-start.6 = ((bf16[32,1,20,1024]{3,2,1,0:T(8,128)(2,1)}), bf16[32,1,20,1024]{3,2,1,0:T(8,128)(2,1)}, u32[]{:S(2)}, u32[]{:S(2)}) async-start(bf16[32,1,20,1024]{3,2,1,0:T(8,128)(2,1)} %bitcast.1411), calls=%async_computation.6 | async-start | bytes 3145728 | tf_op jit(solution)/shard_map/all_to_all | solution.py:207
  506.2 8.1 copy-start.17
  519.2 30.9 %copy-start.22 = (f32[2,64,1024]{2,1,0:T(8,128)}, f32[2,64,1024]{2,1,0:T(8,128)S(1)}, u32[]{:S(2)}) copy-start(f32[2,64,1024]{2,1,0:T(8,128)S(1)} %bitcast_dynamic-update-slice_fusion.18) | copy-start | bytes 1572868
  519.3 57.7 %copy-start.242 = (f32[64]{0:T(128)}, f32[64]{0:T(128)S(1)}, u32[]{:S(2)}) copy-start(f32[64]{0:T(128)S(1)} %fusion.282) | copy-start | bytes 772
  542.9 20.6 %slice-start.2 = ((s8[8388608]{0:T(1024)(128)(4,1)}), s8[4194304]{0:T(1024)(128)(4,1)S(1)}, s32[]{:S(2)}) async-start(s8[8388608]{0:T(1024)(128)(4,1)} %bitcast.1397), calls=%async_computation.36 | async-start | bytes 8388608
  551.3 12.2 slice-start.3
  568.0 35.6 %all-to-all-start.7 = ((bf16[8,4,20,1024]{3,0,2,1:T(8,128)(2,1)}), bf16[8,4,20,1024]{3,0,2,1:T(8,128)(2,1)}, u32[]{:S(2)}, u32[]{:S(2)}) async-start(bf16[8,4,20,1024]{3,0,2,1:T(8,128)(2,1)} %copy.455), calls=%async_computation.7 | async-start | bytes 2621440 | tf_op jit(solution)/shard_map/all_to_all | solution.py:219
  580.3 33.6 %copy-start.170 = (f32[64,32]{0,1:T(8,128)}, f32[64,32]{0,1:T(8,128)S(1)}, u32[]{:S(2)}) copy-start(f32[64,32]{0,1:T(8,128)S(1)} %select_reduce_fusion.2) | copy-start | bytes 24580
  615.2 96.2 %copy-start.79 = (bf16[2,64,1024]{2,1,0:T(8,128)(2,1)}, bf16[2,64,1024]{2,1,0:T(8,128)(2,1)S(1)}, u32[]{:S(2)}) copy-start(bf16[2,64,1024]{2,1,0:T(8,128)(2,1)S(1)} %get-tuple-element.94) | copy-start | bytes 786436
  625.0 87.1 %copy-start.240 = (f32[64]{0:T(128)}, f32[64]{0:T(128)S(1)}, u32[]{:S(2)}) copy-start(f32[64]{0:T(128)S(1)} %get-tuple-element.71) | copy-start | bytes 772
  625.8 3.4 collective-permute-start.2
  638.5 42.1 %all-to-all-start.8 = ((bf16[32,1,20,1024]{3,2,1,0:T(8,128)(2,1)}), bf16[32,1,20,1024]{3,2,1,0:T(8,128)(2,1)}, u32[]{:S(2)}, u32[]{:S(2)}) async-start(bf16[32,1,20,1024]{3,2,1,0:T(8,128)(2,1)} %bitcast.1414), calls=%async_computation.8 | async-start | bytes 3145728 | tf_op jit(solution)/shard_map/all_to_all | solution.py:207
  705.6 35.8 %all-to-all-start.9 = ((bf16[8,4,20,1024]{3,0,2,1:T(8,128)(2,1)}), bf16[8,4,20,1024]{3,0,2,1:T(8,128)(2,1)}, u32[]{:S(2)}, u32[]{:S(2)}) async-start(bf16[8,4,20,1024]{3,0,2,1:T(8,128)(2,1)} %copy.469), calls=%async_computation.9 | async-start | bytes 2621440 | tf_op jit(solution)/shard_map/all_to_all | solution.py:219
  712.1 39.6 %copy-start.172 = (f32[64,32]{0,1:T(8,128)}, f32[64,32]{0,1:T(8,128)S(1)}, u32[]{:S(2)}) copy-start(f32[64,32]{0,1:T(8,128)S(1)} %select_reduce_fusion.1) | copy-start | bytes 24580
  763.6 3.4 collective-permute-start.3
  776.3 42.4 %all-to-all-start.10 = ((bf16[32,1,20,1024]{3,2,1,0:T(8,128)(2,1)}), bf16[32,1,20,1024]{3,2,1,0:T(8,128)(2,1)}, u32[]{:S(2)}, u32[]{:S(2)}) async-start(bf16[32,1,20,1024]{3,2,1,0:T(8,128)(2,1)} %bitcast.1415), calls=%async_computation.10 | async-start | bytes 3145728 | tf_op jit(solution)/shard_map/all_to_all | solution.py:207
  842.0 35.6 %all-to-all-start.11 = ((bf16[8,4,20,1024]{3,0,2,1:T(8,128)(2,1)}), bf16[8,4,20,1024]{3,0,2,1:T(8,128)(2,1)}, u32[]{:S(2)}, u32[]{:S(2)}) async-start(bf16[8,4,20,1024]{3,0,2,1:T(8,128)(2,1)} %copy.483), calls=%async_computation.11 | async-start | bytes 2621440 | tf_op jit(solution)/shard_map/all_to_all | solution.py:219
  846.4 93.2 %reduce-scatter.18.cloned.1.call-start = ((), (), s32[]{:S(2)}) async-start(), calls=%async_computation.21 | async-start | bytes 2621440 | tf_op jit(solution)/shard_map/reduce_scatter | solution.py:415
  848.8 28.8 %copy-start.78 = (bf16[2,64,1024]{2,1,0:T(8,128)(2,1)}, bf16[2,64,1024]{2,1,0:T(8,128)(2,1)S(1)}, u32[]{:S(2)}) copy-start(bf16[2,64,1024]{2,1,0:T(8,128)(2,1)S(1)} %select_dynamic-update-slice_fusion.6) | copy-start | bytes 786436
  848.9 39.0 %copy-start.174 = (f32[64,32]{0,1:T(8,128)}, f32[64,32]{0,1:T(8,128)S(1)}, u32[]{:S(2)}) copy-start(f32[64,32]{0,1:T(8,128)S(1)} %select_reduce_fusion) | copy-start | bytes 24580
  901.2 12.0 copy-start.71
  901.2 72.4 %reduce-scatter.20.cloned.1.call-start = ((), (), s32[]{:S(2)}) async-start(), calls=%async_computation.22 | async-start | bytes 2621440 | tf_op jit(solution)/shard_map/reduce_scatter | solution.py:418
  919.1 92.5 %reduce-scatter.22.cloned.1.call-start = ((), (), s32[]{:S(2)}) async-start(), calls=%async_computation.23 | async-start | bytes 2621440 | tf_op jit(solution)/shard_map/reduce_scatter | solution.py:421
  923.7 181.1 %reduce-scatter.28.cloned.1.call-start = ((), (), s32[]{:S(2)}) async-start(), calls=%async_computation.29 | async-start | bytes 327680
  932.6 173.2 %reduce-scatter.30.cloned.1.call-start = ((), (), s32[]{:S(2)}) async-start(), calls=%async_computation.30 | async-start | bytes 327680
  933.6 173.1 %reduce-scatter.24.cloned.1.call-start = ((), (), s32[]{:S(2)}) async-start(), calls=%async_computation.24 | async-start | bytes 81920 | tf_op jit(solution)/shard_map/reduce_scatter | solution.py:427
  935.5 230.7 %all-reduce.19.cloned.1.call-start = ((), (), s32[]{:S(2)}) async-start(), calls=%async_computation.33 | async-start | bytes 3145728 | tf_op jit(solution)/shard_map/psum | solution.py:433
  939.6 72.1 %copy-start.49 = (bf16[2,8,4,20,512]{4,3,2,1,0:T(8,128)(2,1)S(1)}, bf16[2,8,4,20,512]{4,3,2,1,0:T(8,128)(2,1)}, u32[]{:S(2)}) copy-start(bf16[2,8,4,20,512]{4,3,2,1,0:T(8,128)(2,1)} %get-tuple-element.84) | copy-start | bytes 3932164
  1011.6 243.0 %reduce-scatter.32.cloned.1.call-start = ((), (), s32[]{:S(2)}) async-start(), calls=%async_computation.31 | async-start | bytes 10485760
  1048.6 295.7 %reduce-scatter.34.cloned.1.call-start = ((), (), s32[]{:S(2)}) async-start(), calls=%async_computation.32 | async-start | bytes 10485760
  1086.7 347.1 %reduce-scatter.26.cloned.1.call-start = ((), (), s32[]{:S(2)}) async-start(), calls=%async_computation.25 | async-start | bytes 10485760 | tf_op jit(solution)/shard_map/reduce_scatter | solution.py:446
  1104.8 24.5 %copy-start.143 = (f32[1,2,1,64,1024]{4,3,2,1,0:T(8,128)}, f32[1,2,1,64,1024]{4,3,2,1,0:T(8,128)S(1)}, u32[]{:S(2)}) copy-start(f32[1,2,1,64,1024]{4,3,2,1,0:T(8,128)S(1)} %fusion.244) | copy-start | bytes 1572868
  (222 other events, 730.5 us)
Sparse Core Ops, SparseCore 0:
  9.9 38.0 all-gather.6
  49.8 35.2 all-gather.8
  87.0 35.2 all-gather.10
  901.3 33.3 reduce-scatter.17
  938.4 35.1 reduce-scatter.19
  976.4 35.1 reduce-scatter.21
  1015.2 24.0 reduce-scatter.27
  1042.0 24.0 reduce-scatter.29
  1069.1 23.6 reduce-scatter.23
  1095.2 70.9 all-reduce.18
  1169.2 85.3 reduce-scatter.31
  1257.9 86.4 reduce-scatter.33
  1347.4 86.3 reduce-scatter.25
where the time goes:
time: 1460 us; the launch traced here: 1440 us
  waiting for transfers between devices  756 us (52%)
  local copies, waits for them, and re-layouts  278 us (19%)
  matrix products  191 us (13%)
  other arithmetic  120 us (8%)
  starting transfers between devices  61.1 us (4%)
  blocking collectives  20.8 us (1%)
  between operations  18.2 us (1%)
    unnamed x17, waiting for transfers between devices  166 us
    unnamed x522, local copies, waits for them, and re-layouts  104 us
    all_to_all x3, waiting for transfers between devices, backward_layer(): lax.all_to_all(outgoing, 'expert', split_axis=0, concat_axis=1, tiled=True)  88.1 us
    all_to_all x3, waiting for transfers between devices, backward_layer(): lax.all_to_all(rows_grad, 'expert', split_axis=1, concat_axis=0, tiled=True)  81.2 us
    all_to_all x3, waiting for transfers between devices, forward_layer(): lax.all_to_all(outgoing, 'expert', split_axis=0, concat_axis=1, tiled=True)  80.9 us
    reduce_scatter x1, waiting for transfers between devices, on_device(): lax.psum_scatter(down_grad[None].astype(jnp.bfloat16), 'dp', scatter_dime...  79.5 us
    dynamic_update_slice x48, other arithmetic, store_micro(): lax.dynamic_update_index_in_dim(buffer, jnp.where(active, new_value, prev...  53.9 us
    all_to_all x3, waiting for transfers between devices, forward_layer(): lax.all_to_all(produced, 'expert', split_axis=1, concat_axis=0, tiled=True)  51 us
  transfers between devices with their start and end apart: 29, of which 23 were waited for; matrix products, arithmetic and copies ran while one was open for 19% of the time, Pallas kernels for 0%

commit v1 on v0

v1 whole, which is shorter than its diff:
```python
import jax
import jax.numpy as jnp
from jax import lax
from jax.sharding import PartitionSpec as P

QUERY_HEADS = 16
KEY_VALUE_HEADS = 8
HEAD_DIMENSION = 64
EXPERTS = 32


epsilon = 1e-06
rope_base = 10000.0
highest = lax.Precision.HIGHEST


def normed(values_in, gain_vec):
    return (
        values_in
        * lax.rsqrt(jnp.mean(values_in * values_in, axis=-1, keepdims=True) + epsilon)
        * gain_vec
    )


def rotary_embed(values_in, token_position):
    half_dim = values_in.shape[-1] // 2
    frequency = rope_base ** (-jnp.arange(half_dim, dtype=jnp.float32) / half_dim)
    angles = token_position.astype(jnp.float32)[..., None, None] * frequency
    cosine = jnp.cos(angles)
    sine_part = jnp.sin(angles)
    leading = values_in[..., :half_dim]
    trailing = values_in[..., half_dim:]
    return jnp.concatenate(
        [leading * cosine - trailing * sine_part, trailing * cosine + leading * sine_part], axis=-1
    )


def positions(segment):
    earlier = jnp.sum((segment[..., None, :] < segment[..., :, None]).astype(jnp.int32), axis=-1)
    return jnp.arange(segment.shape[-1], dtype=jnp.int32) - earlier


def causal(segment):
    order_idx = jnp.arange(segment.shape[-1], dtype=jnp.int32)
    return (segment[..., :, None] == segment[..., None, :]) & (
        order_idx[None, :] <= order_idx[:, None]
    )


def attention_scores(query_matrix, key_matrix, allowed):
    sequence_length = query_matrix.shape[0]
    grouped_queries = query_matrix.reshape(
        sequence_length, KEY_VALUE_HEADS, QUERY_HEADS // KEY_VALUE_HEADS, HEAD_DIMENSION
    )
    scores = jnp.einsum(
        "qhgd,khd->hgqk", grouped_queries, key_matrix, preferred_element_type=jnp.float32
    ) * HEAD_DIMENSION ** (-0.5)
    return jnp.where(allowed[None, None], scores, -1e30)


everyone = ("dp", "expert")


def both_layers(block):
    return lax.all_gather(block, "pipe", axis=0, tiled=False)


def rows_of_all(block):
    return lax.all_gather(block, everyone, axis=0, tiled=True)


def summed_rows(block):
    return lax.psum_scatter(block, everyone, scatter_dimension=0, tiled=True)


def dot32(left, right):
    return jnp.dot(left, right, preferred_element_type=jnp.float32)


def expand_matrix(local_experts, slice_width, first_expert):
    column = jnp.arange(4 * EXPERTS)[:, None]
    owner = first_expert + jnp.arange(local_experts * slice_width)[None, :] // slice_width
    return ((column % EXPERTS == owner) & (column < 2 * EXPERTS)).astype(jnp.bfloat16)


def collect_matrix(local_experts, slice_width, first_expert, part, parts):
    column = jnp.arange(parts * EXPERTS)[None, :]
    owner = first_expert + jnp.arange(local_experts * slice_width)[:, None] // slice_width
    return (column == part * EXPERTS + owner).astype(jnp.float32)


def forward_layer(stream, segment, routing, attention, gains, router, experts, expand):
    full_query_keyval, full_out = attention
    gain_attn, gain_ffn = gains
    gate_w, up_w, down_w = experts
    sequence_length, model_width = stream.shape
    attn_normed = normed(stream, gain_attn).astype(jnp.bfloat16)
    query_width = QUERY_HEADS * HEAD_DIMENSION
    split_index = KEY_VALUE_HEADS * HEAD_DIMENSION
    linear = dot32(attn_normed, full_query_keyval)
    query_lin = linear[:, :query_width]
    key_value_linear = linear[:, query_width:]
    token_position = positions(segment)
    query_matrix = rotary_embed(
        query_lin.reshape(sequence_length, QUERY_HEADS, HEAD_DIMENSION), token_position
    ).astype(jnp.bfloat16)
    key_matrix = rotary_embed(
        key_value_linear[:, :split_index].reshape(sequence_length, KEY_VALUE_HEADS, HEAD_DIMENSION),
        token_position,
    ).astype(jnp.bfloat16)
    value_matrix = (
        key_value_linear[:, split_index:]
        .reshape(sequence_length, KEY_VALUE_HEADS, HEAD_DIMENSION)
        .astype(jnp.bfloat16)
    )
    scores = attention_scores(query_matrix, key_matrix, causal(segment))
    row_peak = jnp.max(scores, axis=-1, keepdims=True)
    exponent = jnp.exp(scores - row_peak)
    totals = jnp.sum(exponent, axis=-1, keepdims=True)
    attend_prob = exponent / totals
    attended = jnp.einsum(
        "hgqk,khd->qhgd",
        attend_prob.astype(jnp.bfloat16),
        value_matrix,
        preferred_element_type=jnp.float32,
    )
    attended = attended.reshape(sequence_length, QUERY_HEADS * HEAD_DIMENSION).astype(jnp.bfloat16)
    middle = stream + dot32(attended, full_out)
    ffn_normed = normed(middle, gain_ffn).astype(jnp.bfloat16)
    logits = dot32(ffn_normed, router)
    choose = (routing[:, :, None] == jnp.arange(EXPERTS, dtype=jnp.int32)).astype(jnp.float32)
    gates = jax.nn.softmax(jnp.sum(choose * logits[:, None, :], axis=-1), axis=-1)
    gate_matrix = jnp.sum(choose * gates[:, :, None], axis=1)
    gate_high = lax.reduce_precision(gate_matrix, 8, 7)
    gate_rest = gate_matrix - gate_high
    sent = jnp.concatenate(
        [
            ffn_normed,
            gate_high.astype(jnp.bfloat16),
            gate_rest.astype(jnp.bfloat16),
            jnp.zeros((sequence_length, 2 * EXPERTS), jnp.bfloat16),
        ],
        axis=1,
    )
    arrived = rows_of_all(sent)
    token_rows = arrived[:, :model_width]
    spread_gates = dot32(arrived[:, model_width:], expand)
    gate_lin = dot32(token_rows, gate_w)
    up_lin = dot32(token_rows, up_w)
    inner_act = (jax.nn.silu(gate_lin) * up_lin).astype(jnp.bfloat16)
    weighted = (inner_act.astype(jnp.float32) * spread_gates).astype(jnp.bfloat16)
    mixture = summed_rows(dot32(weighted, down_w).astype(jnp.bfloat16))
    retained = (
        stream,
        attn_normed,
        query_matrix,
        key_matrix,
        value_matrix,
        attend_prob,
        attended,
        middle,
        ffn_normed,
        choose,
        gates,
        token_rows,
        spread_gates,
        gate_lin,
        up_lin,
        inner_act,
        weighted,
    )
    return (middle + mixture.astype(jnp.float32), retained)


def backward_layer(
    carried, retained, segment, attention, gains, router, experts, collect
):
    full_query_keyval, full_out = attention
    gain_attn, gain_ffn = gains
    gate_w, up_w, down_w = experts
    (
        stream,
        attn_normed,
        query_matrix,
        key_matrix,
        value_matrix,
        attend_prob,
        attended,
        middle,
        ffn_normed,
        choose,
        gates,
        token_rows,
        spread_gates,
        gate_lin,
        up_lin,
        inner_act,
        weighted,
    ) = retained
    sequence_length, model_width = carried.shape
    carried_rows = rows_of_all(carried.astype(jnp.bfloat16))
    plain_grad = jnp.einsum("td,fd->tf", carried_rows, down_w, preferred_element_type=jnp.float32)
    choice_grads = jnp.dot(
        inner_act.astype(jnp.float32) * plain_grad, collect, precision=highest
    )
    inner_grad = spread_gates * plain_grad
    squashed = jax.nn.sigmoid(gate_lin)
    gate_low = (inner_grad * up_lin * squashed * (1.0 + gate_lin * (1.0 - squashed))).astype(
        jnp.bfloat16
    )
    up_low = (inner_grad * gate_lin * squashed).astype(jnp.bfloat16)
    row_grads = jnp.einsum("tf,df->td", gate_low, gate_w, preferred_element_type=jnp.float32)
    row_grads = row_grads + jnp.einsum(
        "tf,df->td", up_low, up_w, preferred_element_type=jnp.float32
    )
    returned = summed_rows(
        jnp.concatenate(
            [row_grads.astype(jnp.bfloat16), choice_grads.astype(jnp.bfloat16)], axis=1
        )
    ).astype(jnp.float32)
    expert_grads = (
        jnp.einsum("td,tf->df", token_rows, gate_low, preferred_element_type=jnp.float32),
        jnp.einsum("td,tf->df", token_rows, up_low, preferred_element_type=jnp.float32),
        jnp.einsum("tf,td->fd", weighted, carried_rows, preferred_element_type=jnp.float32),
    )
    expert_grads = tuple(grad.astype(jnp.bfloat16) for grad in expert_grads)
    all_choices = jnp.sum(
        returned[:, model_width:].reshape(sequence_length, -1, EXPERTS), axis=1
    )
    gate_grad = jnp.sum(choose * all_choices[:, None, :], axis=-1)
    chosen_grad = gates * (gate_grad - jnp.sum(gates * gate_grad, axis=-1, keepdims=True))
    logit_grad = jnp.sum(choose * chosen_grad[:, :, None], axis=1)
    router_grad = jnp.einsum(
        "sd,se->de", ffn_normed.astype(jnp.float32), logit_grad, precision=highest
    )
    ffn_grad = jnp.einsum("se,de->sd", logit_grad, router.astype(jnp.float32), precision=highest)
    ffn_grad = ffn_grad + returned[:, :model_width]
    middle_grad, gain_ffn_grad = jax.vjp(normed, middle, gain_ffn)[1](ffn_grad)
    middle_grad = middle_grad + carried
    branch_grad = middle_grad.astype(jnp.bfloat16)
    attention_output_grad = jnp.einsum(
        "sd,ed->se", branch_grad, full_out, preferred_element_type=jnp.float32
    ).astype(jnp.bfloat16)
    query_group_size = QUERY_HEADS // KEY_VALUE_HEADS
    grouped_gradient = attention_output_grad.reshape(
        sequence_length, KEY_VALUE_HEADS, query_group_size, HEAD_DIMENSION
    )
    prob_grad = jnp.einsum(
        "qhgd,khd->hgqk", grouped_gradient, value_matrix, preferred_element_type=jnp.float32
    )
    score_grad = (
        attend_prob * (prob_grad - jnp.sum(prob_grad * attend_prob, axis=-1, keepdims=True))
    ).astype(jnp.bfloat16)
    grouped_queries = query_matrix.reshape(
        sequence_length, KEY_VALUE_HEADS, query_group_size, HEAD_DIMENSION
    )
    query_grad = jnp.einsum(
        "hgqk,khd->qhgd", score_grad, key_matrix, preferred_element_type=jnp.float32
    ).reshape(sequence_length, QUERY_HEADS, HEAD_DIMENSION) * HEAD_DIMENSION ** (-0.5)
    key_gradient = jnp.einsum(
        "hgqk,qhgd->khd", score_grad, grouped_queries, preferred_element_type=jnp.float32
    ) * HEAD_DIMENSION ** (-0.5)
    value_gradient = jnp.einsum(
        "hgqk,qhgd->khd",
        attend_prob.astype(jnp.bfloat16),
        grouped_gradient,
        preferred_element_type=jnp.float32,
    )
    back_position = -positions(segment)
    lows = jnp.concatenate(
        [
            rotary_embed(query_grad, back_position).reshape(sequence_length, -1),
            rotary_embed(key_gradient, back_position).reshape(sequence_length, -1),
            value_gradient.reshape(sequence_length, -1),
        ],
        axis=1,
    ).astype(jnp.bfloat16)
    normed_grad = jnp.einsum(
        "se,de->sd", lows, full_query_keyval, preferred_element_type=jnp.float32
    )
    stream_grad, gain_attn_grad = jax.vjp(normed, stream, gain_attn)[1](normed_grad)
    shared = jnp.concatenate(
        [
            jnp.einsum("sd,se->de", attn_normed, lows, preferred_element_type=jnp.float32),
            jnp.einsum("se,sd->ed", attended, branch_grad, preferred_element_type=jnp.float32),
            router_grad,
            gain_attn_grad[:, None],
            gain_ffn_grad[:, None],
            jnp.zeros((model_width, 128 - EXPERTS - 2), jnp.float32),
        ],
        axis=1,
    ).astype(jnp.bfloat16)
    return (stream_grad + middle_grad, shared, expert_grads)


def on_device(
    inputs,
    cotangent,
    segments,
    routes,
    norm_attn,
    w_query,
    key_value_weight,
    w_out,
    norm_ffn,
    w_router,
    w_gate,
    w_up,
    w_down,
):
    layers = lax.axis_size("pipe")
    core = lax.axis_index("pipe")
    part = lax.axis_index("dp")
    parts = lax.axis_size("dp")
    local_experts, model_width, hidden_units = w_gate.shape[1:]
    slice_width = hidden_units // parts
    first_expert = lax.axis_index("expert") * local_experts

    def own(block, axis=0):
        return lax.dynamic_index_in_dim(block, core, axis, keepdims=False)

    stream = own(inputs)[0].astype(jnp.float32)
    carried = own(cotangent)[0].astype(jnp.float32)
    segment = own(segments)[0]
    routing = own(both_layers(routes[0]), 1)[:, 0]
    gains = both_layers(jnp.concatenate([norm_attn, norm_ffn], axis=0))
    router = both_layers(w_router[0])
    query_keyval = both_layers(
        lax.all_gather(
            jnp.concatenate([w_query[0], key_value_weight[0]], axis=1), "dp", axis=0, tiled=True
        )
    )
    out_full = both_layers(lax.all_gather(w_out[0], "dp", axis=0, tiled=True))

    def columns(weight):
        piece = lax.dynamic_slice_in_dim(weight[0], part * slice_width, slice_width, 2)
        return piece.transpose(1, 0, 2).reshape(model_width, local_experts * slice_width)

    down_piece = lax.dynamic_slice_in_dim(w_down[0], part * slice_width, slice_width, 1)
    gate_all = both_layers(columns(w_gate))
    up_all = both_layers(columns(w_up))
    down_all = both_layers(down_piece.reshape(local_experts * slice_width, model_width))
    expand = expand_matrix(local_experts, slice_width, first_expert)
    collect = collect_matrix(local_experts, slice_width, first_expert, part, parts)

    def params(layer):
        return (
            (query_keyval[layer], out_full[layer]),
            (gains[layer, 0], gains[layer, 1]),
            router[layer],
            (gate_all[layer], up_all[layer], down_all[layer]),
        )

    results, kept = [], []
    for layer in range(layers):
        stream, retained = forward_layer(stream, segment, routing[layer], *params(layer), expand)
        results.append(stream)
        kept.append(retained)
    grads_in, totals = [None] * layers, [None] * layers
    for layer in reversed(range(layers)):
        carried, shared, expert_grads = backward_layer(
            carried, kept[layer], segment, *params(layer), collect
        )
        grads_in[layer] = carried
        leaves = (shared,) + expert_grads
        totals[layer] = [
            leaf.astype(jnp.float32)
            + lax.ppermute(
                leaf, "pipe", [(other, layer) for other in range(layers) if other != layer]
            ).astype(jnp.float32)
            for leaf in leaves
        ]
    shared, gate_grad, up_grad, down_grad = [
        jnp.where(core == 0, first, second) for first, second in zip(*totals)
    ]
    shared = lax.psum_scatter(
        shared.astype(jnp.bfloat16), "dp", scatter_dimension=0, tiled=True
    )
    shared = lax.psum(shared, "expert").astype(jnp.float32)

    def swap(first, second):
        ours = jnp.where(core == 0, first, second)
        theirs = lax.ppermute(
            jnp.where(core == 0, second, first).astype(jnp.bfloat16), "pipe", [(0, 1), (1, 0)]
        ).astype(jnp.float32)
        return jnp.stack(
            [jnp.where(core == 0, ours, theirs), jnp.where(core == 0, theirs, ours)]
        )

    def expert_layout(grad):
        return grad.reshape(model_width, local_experts, slice_width).transpose(1, 0, 2)[None]

    width = model_width
    return (
        swap(*results)[None, :, None],
        swap(*grads_in)[None, :, None],
        shared[None, :, 3 * width + EXPERTS],
        shared[None, :, :width],
        shared[None, :, width : 2 * width],
        shared[None, :, 2 * width : 3 * width],
        shared[None, :, 3 * width + EXPERTS + 1],
        shared[None, :, 3 * width : 3 * width + EXPERTS],
        expert_layout(gate_grad),
        expert_layout(up_grad),
        down_grad.reshape(1, local_experts, slice_width, model_width),
    )


def solution(mesh):
    return jax.shard_map(
        on_device,
        mesh=mesh,
        in_specs=(
            P(None, ("dp", "expert"), None, None),
            P(None, ("dp", "expert"), None, None),
            P(None, ("dp", "expert"), None),
            P("pipe", None, ("dp", "expert"), None, None),
            P("pipe", None),
            P("pipe", "dp", None),
            P("pipe", "dp", None),
            P("pipe", "dp", None),
            P("pipe", None),
            P("pipe", None, None),
            P("pipe", "expert", None, None),
            P("pipe", "expert", None, None),
            P("pipe", "expert", None, None),
        ),
        out_specs=(
            P("pipe", None, ("dp", "expert"), None, None),
            P("pipe", None, ("dp", "expert"), None, None),
            P("pipe", "dp"),
            P("pipe", "dp", None),
            P("pipe", "dp", None),
            P("pipe", "dp", None),
            P("pipe", "dp"),
            P("pipe", "dp", None),
            P("pipe", "expert", None, "dp"),
            P("pipe", "expert", None, "dp"),
            P("pipe", "expert", "dp", None),
        ),
        check_vma=False,
    )
```

time: 1460 us -> 1160 us (0.79)
  local copies, waits for them, and re-layouts: 278 us -> 78.1 us
  other arithmetic: 120 us -> 52.6 us
  waiting for transfers between devices: 756 us -> 823 us
  matrix products: 191 us -> 150 us
  starting transfers between devices: 61.1 us -> 23.7 us
  blocking collectives: 20.8 us -> 5.53 us
    all_to_all x12 -> x0, waiting for transfers between devices: 301 us -> none  [the longest x3 88.1 us: backward_layer(): lax.all_to_all(outgoing, 'expert', split_axis=0, concat_axis=1, tiled=True)]
    reduce_scatter x5, waiting for transfers between devices: 152 us -> 415 us  [the longest x4 385 us: summed_rows(): return lax.psum_scatter(block, everyone, scatter_dimension=0, tiled=True)]
    all_gather x3 -> x11, waiting for transfers between devices: 96.3 us -> 354 us  [the longest x4 208 us: rows_of_all(): return lax.all_gather(block, everyone, axis=0, tiled=True)]
    unnamed x17, waiting for transfers between devices: 166 us -> 0.96 us
    unnamed x522 -> x248, local copies, waits for them, and re-layouts: 104 us -> 13 us
    dynamic_update_slice x48 -> x0, other arithmetic: 53.9 us -> none  [store_micro(): lax.dynamic_update_index_in_dim(buffer, jnp.where(active, new_value, prev...]
    all_to_all x12 -> x0, starting transfers between devices: 53.3 us -> none  [the longest x3 14 us: backward_layer(): lax.all_to_all(outgoing, 'expert', split_axis=0, concat_axis=1, tiled=True)]
    gather x18 -> x0, local copies, waits for them, and re-layouts: 38.6 us -> none  [the longest x9 12.9 us: forward_layer(): jnp.take_along_axis(logits, routing, axis=1)]
  transfers between devices with their start and end apart: 29 -> 27, of which waited for: 23 -> 18; matrix products, arithmetic and copies ran while one was open for 19% -> 18% of each run, Pallas kernels for 0% -> 0%
where the time goes in v1:
time: 1160 us; the launch traced here: 1150 us
  waiting for transfers between devices  823 us (71%)
  matrix products  150 us (13%)
  local copies, waits for them, and re-layouts  78.1 us (7%)
  other arithmetic  52.6 us (5%)
  starting transfers between devices  23.7 us (2%)
  between operations  16.3 us (1%)
    reduce_scatter x4, waiting for transfers between devices, summed_rows(): return lax.psum_scatter(block, everyone, scatter_dimension=0, tiled=True)  385 us
    all_gather x4, waiting for transfers between devices, rows_of_all(): return lax.all_gather(block, everyone, axis=0, tiled=True)  208 us
    dot_general x14, matrix products, dot32(): return jnp.dot(left, right, preferred_element_type=jnp.float32)  56.6 us
    all_gather x1, waiting for transfers between devices, on_device(): lax.all_gather(jnp.concatenate([w_query[0], key_value_weight[0]], axis=1)...  55.5 us
    all_gather x5, waiting for transfers between devices, both_layers(): return lax.all_gather(block, 'pipe', axis=0, tiled=False)  54 us
    psum x1, waiting for transfers between devices, on_device(): shared = lax.psum(shared, 'expert').astype(jnp.float32)  41.8 us
    all_gather x1, waiting for transfers between devices, on_device(): out_full = both_layers(lax.all_gather(w_out[0], 'dp', axis=0, tiled=True))  37.1 us
    reduce_scatter x1, waiting for transfers between devices, on_device(): lax.psum_scatter(shared.astype(jnp.bfloat16), 'dp', scatter_dimension=0,...  29.2 us
  transfers between devices with their start and end apart: 27, of which 18 were waited for; matrix products, arithmetic and copies ran while one was open for 18% of the time, Pallas kernels for 0%

profile of v1, /device:TPU:0, one launch (start us, length us, event | category | flops | bytes accessed | tf_op | source)
XLA Modules:
  0.0 1149.3 jit_solution(9182109599943006883)
XLA Ops:
  10.4 55.5 %all-gather.18.cloned.1.call-done = bf16[1024,2048]{1,0:T(8,128)(2,1)} async-done(((bf16[256,2048]{1,0:T(8,128)(2,1)}), bf16[1024,2048]{1,0:T(8,128)(2,1)}) %all-gather.18.cloned.1.call-update) | async-done | bytes 4194320 | tf_op jit(solution)/shard_map/all_gather | solution.py:329
  66.0 37.1 %all-gather.34.cloned.1.call-done = bf16[1,1024,1024]{2,1,0:T(8,128)(2,1)} async-done(((bf16[1,256,1024]{2,1,0:T(8,128)(2,1)}), bf16[1,1024,1024]{2,1,0:T(8,128)(2,1)}) %all-gather.34.cloned.1.call-update) | async-done | bytes 2097168 | tf_op jit(solution)/shard_map/all_gather | solution.py:333
  110.1 14.4 %all-gather.32.cloned.1.call-done = bf16[2048,2048]{1,0:T(8,128)(2,1)} async-done(((bf16[1024,2048]{1,0:T(8,128)(2,1)}), bf16[2048,2048]{1,0:T(8,128)(2,1)}) %all-gather.32.cloned.1.call-update) | async-done | bytes 8388624 | tf_op jit(solution)/shard_map/all_gather | solution.py:65
  124.5 3.1 fusion.10
  130.7 10.1 all-gather.36.cloned.1.call-done
  146.0 4.7 constant_dynamic-slice_fusion.2
  150.7 2.9 copy.280
  153.5 2.6 copy.281
  156.2 2.9 copy.282
  159.1 2.6 copy.283
  161.7 3.1 constant_dynamic-slice_fusion.1
  165.2 44.4 %all-gather.20.cloned.1.call-done = bf16[1024,1152]{1,0:T(8,128)(2,1)} async-done(((bf16[64,1152]{1,0:T(8,128)(2,1)}), bf16[1024,1152]{1,0:T(8,128)(2,1)}) %all-gather.20.cloned.1.call-update) | async-done | bytes 2359312 | tf_op jit(solution)/shard_map/all_gather | solution.py:69
  209.5 3.8 fusion.61
  213.3 10.7 all-gather.22.cloned.1.call-done
  224.0 6.6 fusion.24
  230.6 10.4 all-gather.24.cloned.1.call-done
  241.0 8.0 multiply_convert_fusion.5
  249.1 8.4 all-gather.26.cloned.1.call-done
  257.4 6.7 convolution_convert_fusion.8
  264.9 85.0 %reduce-scatter.6.cloned.1.call-done = bf16[64,1024]{1,0:T(8,128)(2,1)} async-done(((bf16[1024,1024]{1,0:T(8,128)(2,1)}), bf16[64,1024]{1,0:T(8,128)(2,1)}) %reduce-scatter.6.cloned.1.call-update) | async-done | bytes 131088 | tf_op jit(solution)/shard_map/reduce_scatter | solution.py:73
  351.6 3.1 fusion.6
  363.4 46.5 %all-gather.38.cloned.1.call-done = bf16[1,1,1024,1024]{3,2,1,0:T(8,128)(2,1)} async-done(((bf16[1,1,64,1024]{3,2,1,0:T(8,128)(2,1)}), bf16[1,1,1024,1024]{3,2,1,0:T(8,128)(2,1)}) %all-gather.38.cloned.1.call-update) | async-done | bytes 2097168 | tf_op jit(solution)/shard_map/all_gather | solution.py:69
  409.9 6.5 fusion.16
  416.4 57.2 %all-gather.28.cloned.1.call-done = bf16[1024,1152]{1,0:T(8,128)(2,1)} async-done(((bf16[64,1152]{1,0:T(8,128)(2,1)}), bf16[1024,1152]{1,0:T(8,128)(2,1)}) %all-gather.28.cloned.1.call-update) | async-done | bytes 2359312 | tf_op jit(solution)/shard_map/all_gather | solution.py:69
  475.5 7.4 fusion.31
  483.0 7.6 multiply_convert_fusion.2
  490.6 3.6 convolution_convert_fusion.7
  494.9 4.7 fusion.48
  499.6 2.4 fusion.29
  502.5 2.4 add_convert_fusion.1
  506.6 71.1 %reduce-scatter.8.cloned.1.call-done = bf16[64,1024]{1,0:T(8,128)(2,1)} async-done(((bf16[1024,1024]{1,0:T(8,128)(2,1)}), bf16[64,1024]{1,0:T(8,128)(2,1)}) %reduce-scatter.8.cloned.1.call-update) | async-done | bytes 131088 | tf_op jit(solution)/shard_map/reduce_scatter | solution.py:73
  579.4 128.2 %reduce-scatter.10.cloned.1.call-done = bf16[64,1152]{1,0:T(8,128)(2,1)} async-done(((bf16[1024,1152]{1,0:T(8,128)(2,1)}), bf16[64,1152]{1,0:T(8,128)(2,1)}) %reduce-scatter.10.cloned.1.call-update) | async-done | bytes 147472 | tf_op jit(solution)/shard_map/reduce_scatter | solution.py:73
  710.2 2.4 fusion.58
  718.1 4.3 multiply_reduce_fusion.3
  724.5 59.8 %all-gather.30.cloned.1.call-done = bf16[1024,1024]{1,0:T(8,128)(2,1)} async-done(((bf16[64,1024]{1,0:T(8,128)(2,1)}), bf16[1024,1024]{1,0:T(8,128)(2,1)}) %all-gather.30.cloned.1.call-update) | async-done | bytes 2097168 | tf_op jit(solution)/shard_map/all_gather | solution.py:69
  784.3 9.7 multiply_convert_fusion
  797.7 2.4 fusion.23
  800.1 2.4 add_convert_fusion
  810.4 4.4 convolution_convert_fusion
  814.9 10.5 concatenate.97
  825.4 4.2 collective-permute-start.3
  829.6 101.0 %reduce-scatter.12.cloned.1.call-done = bf16[64,1152]{1,0:T(8,128)(2,1)} async-done(((bf16[1024,1152]{1,0:T(8,128)(2,1)}), bf16[64,1152]{1,0:T(8,128)(2,1)}) %reduce-scatter.12.cloned.1.call-update) | async-done | bytes 147472 | tf_op jit(solution)/shard_map/reduce_scatter | solution.py:73
  947.7 4.3 convolution_convert_fusion.1
  952.0 4.4 fusion.69
  958.2 10.4 concatenate.96
  969.9 11.3 collective-permute-done.2
  981.2 11.1 select_convert_fusion
  994.0 4.2 convolution_convert_fusion.5
  998.2 2.6 collective-permute-start.5
  1000.8 2.4 convolution_convert_fusion.3
  1003.2 2.8 collective-permute-start.7
  1006.0 2.4 convolution_convert_fusion.6
  1010.1 3.7 convolution_convert_fusion.4
  1015.6 3.7 fusion.18
  1019.3 5.9 collective-permute-start.9
  1025.2 3.7 convolution_convert_fusion.2
  1031.0 3.9 add_select_fusion.2
  1035.0 29.2 %reduce-scatter.14.cloned.1.call-done = bf16[256,3200]{1,0:T(8,128)(2,1)} async-done(((bf16[1024,3200]{1,0:T(8,128)(2,1)}), bf16[256,3200]{1,0:T(8,128)(2,1)}) %reduce-scatter.14.cloned.1.call-update) | async-done | bytes 1638416 | tf_op jit(solution)/shard_map/reduce_scatter | solution.py:376
  1064.2 6.8 add_select_fusion.1
  1071.3 7.5 add_select_fusion
  1078.8 5.3 copy.324
  1084.1 5.4 copy.325
  1089.5 5.3 copy.376
  1095.9 41.8 %all-reduce.2.cloned.1.call-done = bf16[256,3200]{1,0:T(8,128)(2,1)} async-done(((bf16[256,3200]{1,0:T(8,128)(2,1)}), bf16[256,3200]{1,0:T(8,128)(2,1)}) %all-reduce.2.cloned.1.call-update) | async-done | bytes 1638416 | tf_op jit(solution)/shard_map/psum | solution.py:379
  (444 shorter events, 90.2 us)
Async XLA Ops:
  7.2 96.0 %copy-start = (s32[2,1,64]{2,1,0:T(1,128)S(1)}, s32[2,1,64]{2,1,0:T(1,128)}, u32[]{:S(2)}) copy-start(s32[2,1,64]{2,1,0:T(1,128)} %param.15) | copy-start | bytes 1540
  7.2 58.7 %all-gather.18.cloned.1.call-start = ((), (), s32[]{:S(2)}) async-start(), calls=%async_computation.5 | async-start | bytes 5242880 | tf_op jit(solution)/shard_map/all_gather | solution.py:329
  9.5 94.7 %copy-start.85 = (s32[1,2,1,64,8]{3,4,2,1,0:T(8,128)S(1)}, s32[1,2,1,64,8]{3,4,2,1,0:T(8,128)}, u32[]{:S(2)}) copy-start(s32[1,2,1,64,8]{3,4,2,1,0:T(8,128)} %param.16) | copy-start | bytes 12292
  9.5 96.6 %copy-start.98 = (f32[1,1024]{1,0:T(1,128)S(1)}, f32[1,1024]{1,0:T(1,128)}, u32[]{:S(2)}) copy-start(f32[1,1024]{1,0:T(1,128)} %param.21) | copy-start | bytes 12292
  9.5 96.6 %copy-start.99 = (f32[1,1024]{1,0:T(1,128)S(1)}, f32[1,1024]{1,0:T(1,128)}, u32[]{:S(2)}) copy-start(f32[1,1024]{1,0:T(1,128)} %param.17) | copy-start | bytes 12292
  9.5 98.4 %copy-start.13 = (bf16[2,1,64,1024]{3,2,1,0:T(8,128)(2,1)S(1)}, bf16[2,1,64,1024]{3,2,1,0:T(8,128)(2,1)}, u32[]{:S(2)}) copy-start(bf16[2,1,64,1024]{3,2,1,0:T(8,128)(2,1)} %param.13) | copy-start | bytes 786436
  9.5 98.5 %copy-start.69 = (bf16[1,1024,32]{1,2,0:T(8,128)(2,1)S(1)}, bf16[1,1024,32]{1,2,0:T(8,128)(2,1)}, u32[]{:S(2)}) copy-start(bf16[1,1024,32]{1,2,0:T(8,128)(2,1)} %param.22) | copy-start | bytes 196612
  9.6 93.5 %all-gather.34.cloned.1.call-start = ((), (), s32[]{:S(2)}) async-start(), calls=%async_computation.19 | async-start | bytes 2621440 | tf_op jit(solution)/shard_map/all_gather | solution.py:333
  10.3 114.2 %all-gather.32.cloned.1.call-start = ((), (), s32[]{:S(2)}) async-start(), calls=%async_computation.18 | async-start | bytes 12582912 | tf_op jit(solution)/shard_map/all_gather | solution.py:65
  65.9 74.9 %all-gather.36.cloned.1.call-start = ((), (), s32[]{:S(2)}) async-start(), calls=%async_computation.20 | async-start | bytes 6291456 | tf_op jit(solution)/shard_map/all_gather | solution.py:65
  103.1 106.4 %all-gather.20.cloned.1.call-start = ((), (), s32[]{:S(2)}) async-start(), calls=%async_computation.6 | async-start | bytes 2506752 | tf_op jit(solution)/shard_map/all_gather | solution.py:69
  110.0 599.6 %copy-start.15 = (bf16[2,1024,32]{1,2,0:T(8,128)(2,1)}, bf16[2,1024,32]{1,2,0:T(8,128)(2,1)S(1)}, u32[]{:S(2)}) copy-start(bf16[2,1024,32]{1,2,0:T(8,128)(2,1)S(1)} %all_gather.60) | copy-start | bytes 393220
  110.0 252.1 %copy-start.62 = (s32[64,8]{0,1:T(8,128)}, s32[64,8]{0,1:T(8,128)S(1)}, u32[]{:S(2)}) copy-start(s32[64,8]{0,1:T(8,128)S(1)} %get-tuple-element.116) | copy-start | bytes 6148
  110.1 247.0 %copy-start.86 = (pred[64,64]{0,1:T(8,128)(4,1)}, pred[64,64]{0,1:T(8,128)(4,1)S(1)}, u32[]{:S(2)}) copy-start(pred[64,64]{0,1:T(8,128)(4,1)S(1)} %fusion.115) | copy-start | bytes 12292
  110.1 250.1 %copy-start.66 = (f32[1,1,1024]{2,1,0:T(1,128)}, f32[1,1,1024]{2,1,0:T(1,128)S(1)}, u32[]{:S(2)}) copy-start(f32[1,1,1024]{2,1,0:T(1,128)S(1)} %get-tuple-element.118) | copy-start | bytes 12292
  145.9 78.1 %all-gather.22.cloned.1.call-start = ((), (), s32[]{:S(2)}) async-start(), calls=%async_computation.7 | async-start | bytes 6291456 | tf_op jit(solution)/shard_map/all_gather | solution.py:65
  156.1 84.9 %all-gather.24.cloned.1.call-start = ((), (), s32[]{:S(2)}) async-start(), calls=%async_computation.8 | async-start | bytes 6291456 | tf_op jit(solution)/shard_map/all_gather | solution.py:65
  161.7 95.8 %all-gather.26.cloned.1.call-start = ((), (), s32[]{:S(2)}) async-start(), calls=%async_computation.9 | async-start | bytes 6291456 | tf_op jit(solution)/shard_map/all_gather | solution.py:65
  164.9 185.1 %reduce-scatter.6.cloned.1.call-start = ((), (), s32[]{:S(2)}) async-start(), calls=%async_computation.10 | async-start | bytes 2228224 | tf_op jit(solution)/shard_map/reduce_scatter | solution.py:73
  264.1 145.7 %all-gather.38.cloned.1.call-start = ((), (), s32[]{:S(2)}) async-start(), calls=%async_computation.21 | async-start | bytes 2228224 | tf_op jit(solution)/shard_map/all_gather | solution.py:69
  264.9 208.7 %all-gather.28.cloned.1.call-start = ((), (), s32[]{:S(2)}) async-start(), calls=%async_computation.11 | async-start | bytes 2506752 | tf_op jit(solution)/shard_map/all_gather | solution.py:69
  357.8 58.6 %copy-start.19 = (bf16[8,64,2,64]{3,1,2,0:T(8,128)(2,1)}, bf16[8,64,2,64]{3,1,2,0:T(8,128)(2,1)S(1)}, u32[]{:S(2)}) copy-start(bf16[8,64,2,64]{3,1,2,0:T(8,128)(2,1)S(1)} %convolution_convert_fusion.11) | copy-start | bytes 393220
  360.2 56.3 %copy-start.103 = (f32[64]{0:T(128)}, f32[64]{0:T(128)S(1)}, u32[]{:S(2)}) copy-start(f32[64]{0:T(128)S(1)} %get-tuple-element.140) | copy-start | bytes 772
  363.1 214.7 %reduce-scatter.8.cloned.1.call-start = ((), (), s32[]{:S(2)}) async-start(), calls=%async_computation.12 | async-start | bytes 2228224 | tf_op jit(solution)/shard_map/reduce_scatter | solution.py:73
  494.3 213.3 %reduce-scatter.10.cloned.1.call-start = ((), (), s32[]{:S(2)}) async-start(), calls=%async_computation.13 | async-start | bytes 2506752 | tf_op jit(solution)/shard_map/reduce_scatter | solution.py:73
  504.8 203.6 %copy-start.63 = (s32[64,8]{0,1:T(8,128)S(1)}, s32[64,8]{0,1:T(8,128)}, u32[]{:S(2)}) copy-start(s32[64,8]{0,1:T(8,128)} %copy-done.62) | copy-start | bytes 6148
  504.8 203.6 %copy-start.78 = (f32[64]{0:T(128)S(1)}, f32[64]{0:T(128)}, u32[]{:S(2)}) copy-start(f32[64]{0:T(128)} %copy-done.77) | copy-start | bytes 772
  504.9 203.6 %copy-start.84 = (f32[64]{0:T(128)S(1)}, f32[64]{0:T(128)}, u32[]{:S(2)}) copy-start(f32[64]{0:T(128)} %copy-done.83) | copy-start | bytes 772
  504.9 204.7 %copy-start.67 = (f32[1,1,1024]{2,1,0:T(1,128)S(1)}, f32[1,1,1024]{2,1,0:T(1,128)}, u32[]{:S(2)}) copy-start(f32[1,1,1024]{2,1,0:T(1,128)} %copy-done.66) | copy-start | bytes 12292
  504.9 204.7 %copy-start.96 = (f32[64]{0:T(128)S(1)}, f32[64]{0:T(128)}, u32[]{:S(2)}) copy-start(f32[64]{0:T(128)} %copy-done.95) | copy-start | bytes 772
  504.9 205.1 %copy-start.104 = (f32[64]{0:T(128)S(1)}, f32[64]{0:T(128)}, u32[]{:S(2)}) copy-start(f32[64]{0:T(128)} %copy-done.103) | copy-start | bytes 772
  506.5 203.5 %copy-start.52 = (bf16[2,1,64,1024]{3,2,1,0:T(8,128)(2,1)S(1)}, bf16[2,1,64,1024]{3,2,1,0:T(8,128)(2,1)}, u32[]{:S(2)}) copy-start(bf16[2,1,64,1024]{3,2,1,0:T(8,128)(2,1)} %param.14) | copy-start | bytes 786436
  506.5 203.5 %copy-start.68 = (f32[1,1,1024]{2,1,0:T(1,128)S(1)}, f32[1,1,1024]{2,1,0:T(1,128)}, u32[]{:S(2)}) copy-start(f32[1,1,1024]{2,1,0:T(1,128)} %copy-done.66) | copy-start | bytes 12292
  506.5 203.5 %copy-start.97 = (f32[64]{0:T(128)S(1)}, f32[64]{0:T(128)}, u32[]{:S(2)}) copy-start(f32[64]{0:T(128)} %copy-done.95) | copy-start | bytes 772
  506.5 206.2 %copy-start.28 = (bf16[64,16,32]{2,0,1:T(8,128)(2,1)S(1)}, bf16[64,16,32]{2,0,1:T(8,128)(2,1)}, u32[]{:S(2)}) copy-start(bf16[64,16,32]{2,0,1:T(8,128)(2,1)} %copy-done.27) | copy-start | bytes 196612
  506.5 206.2 %copy-start.30 = (bf16[64,16,32]{2,0,1:T(8,128)(2,1)S(1)}, bf16[64,16,32]{2,0,1:T(8,128)(2,1)}, u32[]{:S(2)}) copy-start(bf16[64,16,32]{2,0,1:T(8,128)(2,1)} %copy-done.29) | copy-start | bytes 196612
  506.5 206.2 %copy-start.44 = (bf16[64,8,32]{2,0,1:T(8,128)(2,1)S(1)}, bf16[64,8,32]{2,0,1:T(8,128)(2,1)}, u32[]{:S(2)}) copy-start(bf16[64,8,32]{2,0,1:T(8,128)(2,1)} %copy-done.43) | copy-start | bytes 98308
  506.5 206.2 %copy-start.46 = (bf16[64,8,32]{2,0,1:T(8,128)(2,1)S(1)}, bf16[64,8,32]{2,0,1:T(8,128)(2,1)}, u32[]{:S(2)}) copy-start(bf16[64,8,32]{2,0,1:T(8,128)(2,1)} %copy-done.45) | copy-start | bytes 98308
  506.6 206.2 %copy-start.90 = (f32[8,2,64]{2,1,0:T(2,128)S(1)}, f32[8,2,64]{2,1,0:T(2,128)}, u32[]{:S(2)}) copy-start(f32[8,2,64]{2,1,0:T(2,128)} %copy-done.89) | copy-start | bytes 12292
  506.6 277.7 %all-gather.30.cloned.1.call-start = ((), (), s32[]{:S(2)}) async-start(), calls=%async_computation.14 | async-start | bytes 2228224 | tf_op jit(solution)/shard_map/all_gather | solution.py:69
  579.4 135.5 %copy-start.36 = (f32[8,2,64,64]{2,3,1,0:T(8,128)S(1)}, f32[8,2,64,64]{2,3,1,0:T(8,128)}, u32[]{:S(2)}) copy-start(f32[8,2,64,64]{2,3,1,0:T(8,128)} %get-tuple-element.139) | copy-start | bytes 786436
  579.4 143.1 %collective-permute-start = (bf16[64,1024]{1,0:T(8,128)(2,1)}, bf16[64,1024]{1,0:T(8,128)(2,1)}, u32[]{:S(2)}, u32[]{:S(2)}) collective-permute-start(bf16[64,1024]{1,0:T(8,128)(2,1)} %select_convert_fusion.2), channel_id=1, source_target_pairs={{0,16},{16,0},{1,17},{17,1},{2,18},{18,2},{3,19},{19,3},{4,20},{20... | collective-permute-start | bytes 393224 | tf_op jit(solution)/shard_map/ppermute | solution.py:383
  724.3 206.3 %reduce-scatter.12.cloned.1.call-start = ((), (), s32[]{:S(2)}) async-start(), calls=%async_computation.15 | async-start | bytes 2506752 | tf_op jit(solution)/shard_map/reduce_scatter | solution.py:73
  804.2 259.9 %reduce-scatter.14.cloned.1.call-start = ((), (), s32[]{:S(2)}) async-start(), calls=%async_computation.16 | async-start | bytes 8192000 | tf_op jit(solution)/shard_map/reduce_scatter | solution.py:376
  814.9 116.6 %copy-start.61 = (s32[64,8]{0,1:T(8,128)S(1)}, s32[64,8]{0,1:T(8,128)}, u32[]{:S(2)}) copy-start(s32[64,8]{0,1:T(8,128)} %copy-done.60) | copy-start | bytes 6148
  814.9 116.7 %copy-start.76 = (f32[64]{0:T(128)S(1)}, f32[64]{0:T(128)}, u32[]{:S(2)}) copy-start(f32[64]{0:T(128)} %copy-done.75) | copy-start | bytes 772
  814.9 116.7 %copy-start.82 = (f32[64]{0:T(128)S(1)}, f32[64]{0:T(128)}, u32[]{:S(2)}) copy-start(f32[64]{0:T(128)} %copy-done.81) | copy-start | bytes 772
  814.9 117.7 %copy-start.16 = (bf16[2,1024,32]{1,2,0:T(8,128)(2,1)S(1)}, bf16[2,1024,32]{1,2,0:T(8,128)(2,1)}, u32[]{:S(2)}) copy-start(bf16[2,1024,32]{1,2,0:T(8,128)(2,1)} %copy-done.15) | copy-start | bytes 393220
  814.9 117.7 %copy-start.65 = (f32[1,1,1024]{2,1,0:T(1,128)S(1)}, f32[1,1,1024]{2,1,0:T(1,128)}, u32[]{:S(2)}) copy-start(f32[1,1,1024]{2,1,0:T(1,128)} %copy-done.64) | copy-start | bytes 12292
  825.4 112.1 %copy-start.24 = (bf16[64,16,32]{2,0,1:T(8,128)(2,1)S(1)}, bf16[64,16,32]{2,0,1:T(8,128)(2,1)}, u32[]{:S(2)}) copy-start(bf16[64,16,32]{2,0,1:T(8,128)(2,1)} %copy-done.23) | copy-start | bytes 196612
  825.4 112.1 %copy-start.26 = (bf16[64,16,32]{2,0,1:T(8,128)(2,1)S(1)}, bf16[64,16,32]{2,0,1:T(8,128)(2,1)}, u32[]{:S(2)}) copy-start(bf16[64,16,32]{2,0,1:T(8,128)(2,1)} %copy-done.25) | copy-start | bytes 196612
  825.4 112.1 %copy-start.38 = (bf16[64,8,32]{2,0,1:T(8,128)(2,1)S(1)}, bf16[64,8,32]{2,0,1:T(8,128)(2,1)}, u32[]{:S(2)}) copy-start(bf16[64,8,32]{2,0,1:T(8,128)(2,1)} %copy-done.37) | copy-start | bytes 98308
  825.4 112.1 %copy-start.41 = (bf16[64,8,32]{2,0,1:T(8,128)(2,1)S(1)}, bf16[64,8,32]{2,0,1:T(8,128)(2,1)}, u32[]{:S(2)}) copy-start(bf16[64,8,32]{2,0,1:T(8,128)(2,1)} %copy-done.40) | copy-start | bytes 98308
  825.4 112.1 %copy-start.88 = (f32[8,2,64]{2,1,0:T(2,128)S(1)}, f32[8,2,64]{2,1,0:T(2,128)}, u32[]{:S(2)}) copy-start(f32[8,2,64]{2,1,0:T(2,128)} %copy-done.87) | copy-start | bytes 12292
  825.4 144.5 %collective-permute-start.3 = (bf16[1024,3200]{1,0:T(8,128)(2,1)}, bf16[1024,3200]{1,0:T(8,128)(2,1)}, u32[]{:S(2)}, u32[]{:S(2)}) collective-permute-start(bf16[1024,3200]{1,0:T(8,128)(2,1)} %concatenate.97), channel_id=1, source_target_pairs={{0,16},{1,17},{2,18},{3,19},{4,20},{5,21},{6,22},{7,23},{8,24},{9,... | collective-permute-start | bytes 19660808 | tf_op jit(solution)/shard_map/ppermute | solution.py:368
  968.6 12.6 %collective-permute-start.2 = (bf16[1024,3200]{1,0:T(8,128)(2,1)}, bf16[1024,3200]{1,0:T(8,128)(2,1)S(1)}, u32[]{:S(2)}, u32[]{:S(2)}) collective-permute-start(bf16[1024,3200]{1,0:T(8,128)(2,1)} %concatenate.96), channel_id=1, source_target_pairs={{16,0},{17,1},{18,2},{19,3},{20,4},{21,5},{22,6},{23,7},{24,8},{25... | collective-permute-start | bytes 19660808 | tf_op jit(solution)/shard_map/ppermute | solution.py:368
  992.4 145.2 %all-reduce.2.cloned.1.call-start = ((), (), s32[]{:S(2)}) async-start(), calls=%async_computation.17 | async-start | bytes 3276800 | tf_op jit(solution)/shard_map/psum | solution.py:379
  998.2 30.7 %collective-permute-start.5 = (bf16[1024,1024]{0,1:T(8,128)(2,1)S(1)}, bf16[1024,1024]{0,1:T(8,128)(2,1)S(1)}, u32[]{:S(2)}, u32[]{:S(2)}) collective-permute-start(bf16[1024,1024]{0,1:T(8,128)(2,1)S(1)} %convolution_convert_fusion.5), channel_id=1, source_target_pairs={{0,16},{1,17},{2,18},{3,19},{4,20},{5,21},{6,22},{7,23},{8,24},{9,... | collective-permute-start | bytes 6291464 | tf_op jit(solution)/shard_map/ppermute | solution.py:368
  1003.2 61.0 %collective-permute-start.7 = (bf16[1024,1024]{0,1:T(8,128)(2,1)S(1)}, bf16[1024,1024]{0,1:T(8,128)(2,1)}, u32[]{:S(2)}, u32[]{:S(2)}) collective-permute-start(bf16[1024,1024]{0,1:T(8,128)(2,1)S(1)} %convolution_convert_fusion.3), channel_id=1, source_target_pairs={{0,16},{1,17},{2,18},{3,19},{4,20},{5,21},{6,22},{7,23},{8,24},{9,... | collective-permute-start | bytes 6291464 | tf_op jit(solution)/shard_map/ppermute | solution.py:368
  1008.5 22.5 %collective-permute-start.4 = (bf16[1024,1024]{0,1:T(8,128)(2,1)S(1)}, bf16[1024,1024]{0,1:T(8,128)(2,1)S(1)}, u32[]{:S(2)}, u32[]{:S(2)}) collective-permute-start(bf16[1024,1024]{0,1:T(8,128)(2,1)S(1)} %convolution_convert_fusion.6), channel_id=1, source_target_pairs={{16,0},{17,1},{18,2},{19,3},{20,4},{21,5},{22,6},{23,7},{24,8},{25... | collective-permute-start | bytes 6291464 | tf_op jit(solution)/shard_map/ppermute | solution.py:368
  1013.8 50.4 %collective-permute-start.6 = (bf16[1024,1024]{0,1:T(8,128)(2,1)}, bf16[1024,1024]{0,1:T(8,128)(2,1)}, u32[]{:S(2)}, u32[]{:S(2)}) collective-permute-start(bf16[1024,1024]{0,1:T(8,128)(2,1)} %convolution_convert_fusion.4), channel_id=1, source_target_pairs={{16,0},{17,1},{18,2},{19,3},{20,4},{21,5},{22,6},{23,7},{24,8},{25... | collective-permute-start | bytes 6291464 | tf_op jit(solution)/shard_map/ppermute | solution.py:368
  1019.3 52.0 %collective-permute-start.9 = (bf16[1024,1024]{0,1:T(8,128)(2,1)}, bf16[1024,1024]{0,1:T(8,128)(2,1)}, u32[]{:S(2)}, u32[]{:S(2)}) collective-permute-start(bf16[1024,1024]{0,1:T(8,128)(2,1)} %fusion.18), channel_id=1, source_target_pairs={{0,16},{1,17},{2,18},{3,19},{4,20},{5,21},{6,22},{7,23},{8,24},{9,... | collective-permute-start | bytes 6291464 | tf_op jit(solution)/shard_map/ppermute | solution.py:368
  1028.9 42.4 %collective-permute-start.8 = (bf16[1024,1024]{0,1:T(8,128)(2,1)}, bf16[1024,1024]{0,1:T(8,128)(2,1)}, u32[]{:S(2)}, u32[]{:S(2)}) collective-permute-start(bf16[1024,1024]{0,1:T(8,128)(2,1)} %convolution_convert_fusion.2), channel_id=1, source_target_pairs={{16,0},{17,1},{18,2},{19,3},{20,4},{21,5},{22,6},{23,7},{24,8},{25... | collective-permute-start | bytes 6291464 | tf_op jit(solution)/shard_map/ppermute | solution.py:368
  1071.2 23.6 %collective-permute-start.1 = (bf16[64,1024]{1,0:T(8,128)(2,1)S(1)}, bf16[64,1024]{1,0:T(8,128)(2,1)S(1)}, u32[]{:S(2)}, u32[]{:S(2)}) collective-permute-start(bf16[64,1024]{1,0:T(8,128)(2,1)S(1)} %select_convert_fusion.1), channel_id=1, source_target_pairs={{0,16},{16,0},{1,17},{17,1},{2,18},{18,2},{3,19},{19,3},{4,20},{20... | collective-permute-start | bytes 393224 | tf_op jit(solution)/shard_map/ppermute | solution.py:383
  (86 other events, 649.0 us)
Sparse Core Ops, SparseCore 0:
  10.4 55.3 all-gather.17
  67.7 35.3 all-gather.33
  104.6 19.8 all-gather.31
  125.9 14.8 all-gather.35
  146.1 63.4 all-gather.19
  211.5 12.4 all-gather.21
  226.1 14.8 all-gather.23
  242.6 14.8 all-gather.25
  264.2 85.6 reduce-scatter.5
  352.6 57.2 all-gather.37
  412.6 60.9 all-gather.27
  494.4 83.3 reduce-scatter.7
  582.7 124.8 reduce-scatter.9
  724.4 59.8 all-gather.29
  804.3 126.2 reduce-scatter.11
  992.5 71.5 reduce-scatter.13
  1066.4 71.2 all-reduce.1

commit v2 on v1

--- a/solution.py
+++ b/solution.py
@@ -58,19 +58,47 @@
     return jnp.where(allowed[None, None], scores, -1e30)
 
 
-everyone = ("dp", "expert")
-
-
 def both_layers(block):
     return lax.all_gather(block, "pipe", axis=0, tiled=False)
 
 
+def layer_pair(block):
+    other = lax.ppermute(block, "pipe", [(0, 1), (1, 0)])
+    first = lax.axis_index("pipe") == 0
+    return jnp.where(first, block, other), jnp.where(first, other, block)
+
+
+def ahead(axis, step):
+    count = lax.axis_size(axis)
+    return [(i, (i + step) % count) for i in range(count)]
+
+
+def across(axis, step):
+    return [(i, i ^ step) for i in range(lax.axis_size(axis))]
+
+
 def rows_of_all(block):
-    return lax.all_gather(block, everyone, axis=0, tiled=True)
+    blocks = [block]
+    for step in range(1, lax.axis_size("expert")):
+        blocks.append(lax.ppermute(block, "expert", ahead("expert", step)))
+    block = jnp.concatenate(blocks, axis=0)
+    blocks = [block]
+    for step in range(1, lax.axis_size("dp")):
+        blocks.append(lax.ppermute(block, "dp", across("dp", step)))
+    return jnp.concatenate(blocks, axis=0)
 
 
 def summed_rows(block):
-    return lax.psum_scatter(block, everyone, scatter_dimension=0, tiled=True)
+    blocks = jnp.split(block, lax.axis_size("dp"), axis=0)
+    total = blocks[0].astype(jnp.float32)
+    for step in range(1, len(blocks)):
+        total = total + lax.ppermute(blocks[step], "dp", across("dp", step)).astype(jnp.float32)
+    blocks = jnp.split(total.astype(jnp.bfloat16), lax.axis_size("expert"), axis=0)
+    total = blocks[0].astype(jnp.float32)
+    for step in range(1, len(blocks)):
+        arrived = lax.ppermute(blocks[step], "expert", ahead("expert", -step))
+        total = total + arrived.astype(jnp.float32)
+    return total
 
 
 def dot32(left, right):
@@ -325,21 +353,21 @@
     routing = own(both_layers(routes[0]), 1)[:, 0]
     gains = both_layers(jnp.concatenate([norm_attn, norm_ffn], axis=0))
     router = both_layers(w_router[0])
-    query_keyval = both_layers(
+    query_keyval = layer_pair(
         lax.all_gather(
             jnp.concatenate([w_query[0], key_value_weight[0]], axis=1), "dp", axis=0, tiled=True
         )
     )
-    out_full = both_layers(lax.all_gather(w_out[0], "dp", axis=0, tiled=True))
+    out_full = layer_pair(lax.all_gather(w_out[0], "dp", axis=0, tiled=True))
 
     def columns(weight):
         piece = lax.dynamic_slice_in_dim(weight[0], part * slice_width, slice_width, 2)
         return piece.transpose(1, 0, 2).reshape(model_width, local_experts * slice_width)
 
     down_piece = lax.dynamic_slice_in_dim(w_down[0], part * slice_width, slice_width, 1)
-    gate_all = both_layers(columns(w_gate))
-    up_all = both_layers(columns(w_up))
-    down_all = both_layers(down_piece.reshape(local_experts * slice_width, model_width))
+    gate_all = layer_pair(columns(w_gate))
+    up_all = layer_pair(columns(w_up))
+    down_all = layer_pair(down_piece.reshape(local_experts * slice_width, model_width))
     expand = expand_matrix(local_experts, slice_width, first_expert)
     collect = collect_matrix(local_experts, slice_width, first_expert, part, parts)
 

time: 1160 us -> 729 us (0.63)
  waiting for transfers between devices: 823 us -> 284 us
  starting transfers between devices: 23.7 us -> 103 us
  local copies, waits for them, and re-layouts: 78.1 us -> 95.6 us
  other arithmetic: 52.6 us -> 66.9 us
    reduce_scatter x4 -> x0, waiting for transfers between devices: 385 us -> none  [summed_rows(): return lax.psum_scatter(block, everyone, scatter_dimension=0, tiled=True)]
    all_gather x10 -> x1, waiting for transfers between devices: 299 us -> 14.5 us  [on_device(): out_full = layer_pair(lax.all_gather(w_out[0], 'dp', axis=0, tiled=True))]
    ppermute x0 -> x53, waiting for transfers between devices: none -> 138 us  [the longest x12 62.5 us: rows_of_all(): blocks.append(lax.ppermute(block, 'dp', across('dp', step)))]
    ppermute x0 -> x53, starting transfers between devices: none -> 80.7 us  [the longest x12 33 us: summed_rows(): arrived = lax.ppermute(blocks[step], 'expert', ahead('expert', -step))]
    transpose x0 -> x3, local copies, waits for them, and re-layouts: none -> 12.5 us  [columns(): piece.transpose(1, 0, 2).reshape(model_width, local_experts * slice_width)]
  transfers between devices with their start and end apart: 27 -> 67, of which waited for: 18 -> 27; matrix products, arithmetic and copies ran while one was open for 18% -> 30% of each run, Pallas kernels for 0% -> 0%
where the time goes in v2:
time: 729 us; the launch traced here: 720 us
  waiting for transfers between devices  284 us (39%)
  matrix products  147 us (20%)
  starting transfers between devices  103 us (14%)
  local copies, waits for them, and re-layouts  95.6 us (13%)
  other arithmetic  66.9 us (9%)
  between operations  16.4 us (2%)
  blocking collectives  7.35 us (1%)
    ppermute x12, waiting for transfers between devices, rows_of_all(): blocks.append(lax.ppermute(block, 'dp', across('dp', step)))  62.5 us
    all_gather x1, waiting for transfers between devices, on_device(): lax.all_gather(jnp.concatenate([w_query[0], key_value_weight[0]], axis=1)...  56.2 us
    ppermute x12, waiting for transfers between devices, summed_rows(): lax.ppermute(blocks[step], 'dp', across('dp', step)).astype(jnp.float32)  47.3 us
    dot_general x14, matrix products, dot32(): return jnp.dot(left, right, preferred_element_type=jnp.float32)  45.6 us
    psum x1, waiting for transfers between devices, on_device(): shared = lax.psum(shared, 'expert').astype(jnp.float32)  34.9 us
    ppermute x12, starting transfers between devices, summed_rows(): arrived = lax.ppermute(blocks[step], 'expert', ahead('expert', -step))  33 us
    reduce_scatter x1, waiting for transfers between devices, on_device(): lax.psum_scatter(shared.astype(jnp.bfloat16), 'dp', scatter_dimension=0,...  28.8 us
    select_n x3, other arithmetic, on_device(): jnp.where(core == 0, first, second)  21.7 us
  transfers between devices with their start and end apart: 67, of which 27 were waited for; matrix products, arithmetic and copies ran while one was open for 30% of the time, Pallas kernels for 0%

profile of v2, /device:TPU:0, one launch (start us, length us, event | category | flops | bytes accessed | tf_op | source)
XLA Modules:
  0.0 720.4 jit_solution(4296663415700200411)
XLA Ops:
  9.7 56.2 %all-gather.6.cloned.1.call-done = bf16[1024,2048]{1,0:T(8,128)(2,1)} async-done(((bf16[256,2048]{1,0:T(8,128)(2,1)}), bf16[1024,2048]{1,0:T(8,128)(2,1)}) %all-gather.6.cloned.1.call-update) | async-done | bytes 4194320 | tf_op jit(solution)/shard_map/all_gather | solution.py:357
  82.3 4.7 dynamic-slice_bitcast_fusion
  89.1 14.5 %all-gather.8.cloned.1.call-done = bf16[1,1024,1024]{1,2,0:T(8,128)(2,1)} async-done(((bf16[1,256,1024]{1,2,0:T(8,128)(2,1)}), bf16[1,1024,1024]{1,2,0:T(8,128)(2,1)}) %all-gather.8.cloned.1.call-update) | async-done | bytes 2097168 | tf_op jit(solution)/shard_map/all_gather | solution.py:361
  104.1 3.7 all_gather.23
  108.0 3.9 copy.285
  111.9 3.9 copy.286
  115.8 4.0 copy.370
  121.8 3.1 fusion.7
  145.1 5.5 collective-permute-done.3
  154.4 12.6 %collective-permute-done.5 = bf16[256,1152]{1,0:T(8,128)(2,1)S(1)} collective-permute-done((bf16[256,1152]{1,0:T(8,128)(2,1)S(1)}, bf16[256,1152]{1,0:T(8,128)(2,1)S(1)}, u32[]{:S(2)}, u32[]{:S(2)}) %collective-permute-start.5) | collective-permute-done | bytes 589856 | tf_op jit(solution)/shard_map/ppermute | solution.py:87
  167.1 11.8 %collective-permute-done.6 = bf16[256,1152]{1,0:T(8,128)(2,1)S(1)} collective-permute-done((bf16[256,1152]{1,0:T(8,128)(2,1)S(1)}, bf16[256,1152]{1,0:T(8,128)(2,1)S(1)}, u32[]{:S(2)}, u32[]{:S(2)}) %collective-permute-start.6) | collective-permute-done | bytes 589856 | tf_op jit(solution)/shard_map/ppermute | solution.py:87
  186.9 4.7 multiply_convert_fusion.5
  197.9 7.2 %collective-permute-done.34 = bf16[256,1024]{1,0:T(8,128)(2,1)S(1)} collective-permute-done((bf16[256,1024]{1,0:T(8,128)(2,1)S(1)}, bf16[256,1024]{1,0:T(8,128)(2,1)S(1)}, u32[]{:S(2)}, u32[]{:S(2)}) %collective-permute-start.34) | collective-permute-done | bytes 524320 | tf_op jit(solution)/shard_map/ppermute | solution.py:87
  205.2 8.5 %collective-permute-done.11 = bf16[256,1024]{1,0:T(8,128)(2,1)S(1)} collective-permute-done((bf16[256,1024]{1,0:T(8,128)(2,1)S(1)}, bf16[256,1024]{1,0:T(8,128)(2,1)S(1)}, u32[]{:S(2)}, u32[]{:S(2)}) %collective-permute-start.11) | collective-permute-done | bytes 524320 | tf_op jit(solution)/shard_map/ppermute | solution.py:95
  213.7 12.4 %collective-permute-done.12 = bf16[256,1024]{1,0:T(8,128)(2,1)S(1)} collective-permute-done((bf16[256,1024]{1,0:T(8,128)(2,1)S(1)}, bf16[256,1024]{1,0:T(8,128)(2,1)S(1)}, u32[]{:S(2)}, u32[]{:S(2)}) %collective-permute-start.12) | collective-permute-done | bytes 524320 | tf_op jit(solution)/shard_map/ppermute | solution.py:95
  226.5 3.7 collective-permute-start.14
  232.1 4.4 fusion.41
  236.5 5.7 collective-permute-done.15
  242.5 3.3 fusion.9
  263.8 3.2 collective-permute-start.19
  269.9 3.5 collective-permute-done.18
  277.2 11.5 %collective-permute-done.20 = bf16[256,1152]{1,0:T(8,128)(2,1)S(1)} collective-permute-done((bf16[256,1152]{1,0:T(8,128)(2,1)S(1)}, bf16[256,1152]{1,0:T(8,128)(2,1)S(1)}, u32[]{:S(2)}, u32[]{:S(2)}) %collective-permute-start.20) | collective-permute-done | bytes 589856 | tf_op jit(solution)/shard_map/ppermute | solution.py:87
  288.8 6.5 collective-permute-done.21
  297.9 7.6 %fusion.12 = f32[1024,1024]{1,0:T(8,128)} fusion(bf16[1024,1152]{1,0:T(8,128)(2,1)S(1)} %constant_dynamic-update-slice_fusion.7, bf16[1024,1024]{0,1:T(8,128)(2,1)} %collective-permute-done.9, bf16[1024,1024]{0,1:T(8,128)(2,1)S(1)} %bitcast.302, pred[]{:T(512)S(6)} %eq.44), kind=kOutput, calls=%fused_computation.66 | convolution fusion | flops 2148532224 | bytes 10485761 | tf_op jit(solution)/shard_map/dot_general | solution.py:105
  305.5 10.5 %multiply_convert_fusion.3 = (bf16[1024,1024]{1,0:T(8,128)(2,1)}, bf16[1024,1024]{1,0:T(8,128)(2,1)}, bf16[1024,1024]{1,0:T(8,128)(2,1)}) fusion(f32[1024,1024]{1,0:T(8,128)} %fusion.12, f32[1024,1024]{1,0:T(8,128)S(1)} %fusion.48, f32[1024,1024]{1,0:T(8,128)S(1)} %copy-done.10, bf16[1024,1024]{0,1:T(8,128)(2,1)} %collective-permute-done.8, ...), kind=kOutput, calls=%fused_computation.19 | convolution fusion | flops 2166358016 | bytes 25165824 | tf_op jit(solution)/shard_map/dot_general | solution.py:105
  316.0 4.6 convolution_convert_fusion.8
  324.4 4.1 fusion.40
  328.5 4.3 add_convert_fusion.1
  338.9 9.4 %collective-permute-done.24 = bf16[256,1024]{1,0:T(8,128)(2,1)S(1)} collective-permute-done((bf16[256,1024]{1,0:T(8,128)(2,1)S(1)}, bf16[256,1024]{1,0:T(8,128)(2,1)S(1)}, u32[]{:S(2)}, u32[]{:S(2)}) %collective-permute-start.24) | collective-permute-done | bytes 524320 | tf_op jit(solution)/shard_map/ppermute | solution.py:95
  348.7 5.4 collective-permute-done.36
  354.0 7.4 %collective-permute-done.37 = bf16[256,1152]{1,0:T(8,128)(2,1)S(1)} collective-permute-done((bf16[256,1152]{1,0:T(8,128)(2,1)S(1)}, bf16[256,1152]{1,0:T(8,128)(2,1)S(1)}, u32[]{:S(2)}, u32[]{:S(2)}) %collective-permute-start.37) | collective-permute-done | bytes 589856 | tf_op jit(solution)/shard_map/ppermute | solution.py:95
  361.8 11.9 %collective-permute-start.39 = (bf16[64,1152]{1,0:T(8,128)(2,1)S(1)}, bf16[64,1152]{1,0:T(8,128)(2,1)S(1)}, u32[]{:S(2)}, u32[]{:S(2)}) collective-permute-start(bf16[64,1152]{1,0:T(8,128)(2,1)S(1)} %get-tuple-element.112), channel_id=1, source_target_pairs={{0,3},{1,0},{2,1},{3,2},{4,7},{5,4},{6,5},{7,6},{8,11},{9,8},{10,9... | collective-permute-start | bytes 442376 | tf_op jit(solution)/shard_map/ppermute | solution.py:99
  375.6 3.7 collective-permute-start.26
  379.4 5.9 collective-permute-start.28
  385.3 3.5 collective-permute-done.40
  406.7 4.4 multiply_reduce_fusion.3
  414.7 3.1 collective-permute-start.44
  425.7 5.6 collective-permute-done.45
  431.3 6.2 collective-permute-done.46
  437.7 7.4 %multiply_convert_fusion.1 = (bf16[1024,1024]{1,0:T(8,128)(2,1)}, bf16[1024,1024]{1,0:T(8,128)(2,1)S(1)}, f32[1024,1024]{1,0:T(8,128)S(1)}) fusion(f32[1024,1024]{1,0:T(8,128)S(1)} %copy-done.136, f32[1024,1024]{1,0:T(8,128)} %get-tuple-element.166, f32[1024,1024]{1,0:T(8,128)S(1)} %copy-done.7, ...), kind=kOutput, calls=%fused_computation.16 | convolution fusion | flops 2163212288 | bytes 27262976 | tf_op jit(solution)/shard_map/td,fd->tf/dot_general | solution.py:230
  463.9 4.6 convolution_convert_fusion
  468.6 4.3 collective-permute-done.49
  475.5 3.8 collective-permute-start.51
  482.3 10.9 %concatenate.133 = bf16[1024,3200]{1,0:T(8,128)(2,1)} concatenate(bf16[1024,2048]{1,0:T(8,128)(2,1)} %convolution_convert_fusion, bf16[1024,1024]{1,0:T(8,128)(2,1)} %convolution_convert_fusion.10, bf16[1024,32]{1,0:T(8,128)(2,1)} %copy.325, bf16[1024,1]{1,0:T(8,128)(2,1)} %broadcast_in_dim.72, bf16[1024,1]{1,0:T(8,128)(2,1)} %broadcast_in_dim.73, bf16[1024,94]{1,0:T(8,128)(2,1)S(1)} %broadcast.494), dimensions={1} | concatenate | bytes 13107200 | tf_op jit(solution)/shard_map/concatenate | solution.py:310
  493.2 3.9 collective-permute-start.56
  519.9 4.5 convolution_convert_fusion.1
  528.5 10.4 %concatenate.132 = bf16[1024,3200]{1,0:T(8,128)(2,1)} concatenate(bf16[1024,2048]{1,0:T(8,128)(2,1)} %convolution_convert_fusion.1, bf16[1024,1024]{1,0:T(8,128)(2,1)S(1)} %convolution_convert_fusion.11, bf16[1024,32]{1,0:T(8,128)(2,1)} %copy.321, bf16[1024,1]{1,0:T(8,128)(2,1)} %broadcast_in_dim.70, bf16[1024,1]{1,0:T(8,128)(2,1)} %broadcast_in_dim.71, ...), dimensions={1} | concatenate | bytes 13107200 | tf_op jit(solution)/shard_map/concatenate | solution.py:310
  540.2 11.3 %collective-permute-done.55 = bf16[1024,3200]{1,0:T(8,128)(2,1)S(1)} collective-permute-done((bf16[1024,3200]{1,0:T(8,128)(2,1)}, bf16[1024,3200]{1,0:T(8,128)(2,1)S(1)}, u32[]{:S(2)}, u32[]{:S(2)}) %collective-permute-start.55) | collective-permute-done | bytes 6553632 | tf_op jit(solution)/shard_map/ppermute | solution.py:396
  551.5 11.1 %select_convert_fusion = bf16[1024,3200]{1,0:T(8,128)(2,1)} fusion(bf16[1024,3200]{1,0:T(8,128)(2,1)} %collective-permute-done.56, bf16[1024,3200]{1,0:T(8,128)(2,1)} %concatenate.133, bf16[1024,3200]{1,0:T(8,128)(2,1)S(1)} %collective-permute-done.55, bf16[1024,3200]{1,0:T(8,128)(2,1)} %concatenate.132, pred[]{:T(512)S(6)} %eq.44), kind=kLoop, calls=%fused_computation.2 | loop fusion | flops 26214400 | bytes 32768000 | tf_op jit(solution)/shard_map/convert_element_type | solution.py:405
  564.2 5.4 convolution_convert_fusion.2
  572.3 3.7 convolution_convert_fusion.4
  581.5 3.8 convolution_convert_fusion.3
  586.9 3.8 convolution_convert_fusion.5
  592.4 3.8 collective-permute-start.54
  596.2 3.7 convolution_convert_fusion.7
  599.9 3.3 collective-permute-start.58
  606.3 28.8 %reduce-scatter.2.cloned.1.call-done = bf16[256,3200]{1,0:T(8,128)(2,1)} async-done(((bf16[1024,3200]{1,0:T(8,128)(2,1)}), bf16[256,3200]{1,0:T(8,128)(2,1)}) %reduce-scatter.2.cloned.1.call-update) | async-done | bytes 1638416 | tf_op jit(solution)/shard_map/reduce_scatter | solution.py:404
  636.0 7.4 %add_select_fusion = f32[1024,1024]{0,1:T(8,128)} fusion(bf16[1024,1024]{0,1:T(8,128)(2,1)} %copy-done.15, bf16[1024,1024]{0,1:T(8,128)(2,1)} %copy-done.14, bf16[1024,1024]{0,1:T(8,128)(2,1)} %collective-permute-done.61, bf16[1024,1024]{0,1:T(8,128)(2,1)} %convolution_convert_fusion.3, pred[]{:T(512)S(6)} %eq.44), kind=kLoop, calls=%fused_computation.11 | loop fusion | flops 7340032 | bytes 12582913 | tf_op jit(solution)/shard_map/jit(_where)/select_n | solution.py:402
  643.4 5.3 copy.381
  648.7 7.4 %add_select_fusion.1 = f32[1024,1024]{0,1:T(8,128)} fusion(bf16[1024,1024]{0,1:T(8,128)(2,1)} %collective-permute-done.60, bf16[1024,1024]{0,1:T(8,128)(2,1)} %convolution_convert_fusion.4, bf16[1024,1024]{0,1:T(8,128)(2,1)} %collective-permute-done.59, bf16[1024,1024]{0,1:T(8,128)(2,1)} %convolution_convert_fusion.5, pred[]{:T(512)S(6)} %eq.44), kind=kLoop, calls=%fused_computation.12 | loop fusion | flops 7340032 | bytes 12582913 | tf_op jit(solution)/shard_map/jit(_where)/select_n | solution.py:402
  656.2 5.3 copy.329
  661.5 6.9 add_select_fusion.2
  668.4 5.4 copy.328
  673.7 34.9 %all-reduce.2.cloned.1.call-done = bf16[256,3200]{1,0:T(8,128)(2,1)} async-done(((bf16[256,3200]{1,0:T(8,128)(2,1)}), bf16[256,3200]{1,0:T(8,128)(2,1)}) %all-reduce.2.cloned.1.call-update) | async-done | bytes 1638416 | tf_op jit(solution)/shard_map/psum | solution.py:407
  (595 shorter events, 206.4 us)
Async XLA Ops:
  7.2 58.7 %all-gather.6.cloned.1.call-start = ((), (), s32[]{:S(2)}) async-start(), calls=%async_computation.1 | async-start | bytes 5242880 | tf_op jit(solution)/shard_map/all_gather | solution.py:357
  9.7 93.9 %all-gather.8.cloned.1.call-start = ((), (), s32[]{:S(2)}) async-start(), calls=%async_computation.4 | async-start | bytes 2621440 | tf_op jit(solution)/shard_map/all_gather | solution.py:361
  65.9 55.9 %collective-permute-start = (bf16[1024,2048]{1,0:T(8,128)(2,1)}, bf16[1024,2048]{1,0:T(8,128)(2,1)}, u32[]{:S(2)}, u32[]{:S(2)}) collective-permute-start(bf16[1024,2048]{1,0:T(8,128)(2,1)} %all-gather.6.cloned.1.call-done), channel_id=1, source_target_pairs={{0,16},{16,0},{1,17},{17,1},{2,18},{18,2},{3,19},{19,3},{4,20},{20... | collective-permute-start | bytes 12582920 | tf_op jit(solution)/shard_map/ppermute | solution.py:66
  66.9 568.2 %reduce-scatter.2.cloned.1.call-start = ((), (), s32[]{:S(2)}) async-start(), calls=%async_computation.2 | async-start | bytes 8192000 | tf_op jit(solution)/shard_map/reduce_scatter | solution.py:404
  67.7 52.1 %collective-permute-start.30 = (bf16[64,1024]{1,0:T(8,128)(2,1)S(1)}, bf16[64,1024]{1,0:T(8,128)(2,1)S(1)}, u32[]{:S(2)}, u32[]{:S(2)}) collective-permute-start(bf16[64,1024]{1,0:T(8,128)(2,1)S(1)} %get-tuple-element.82), channel_id=1, source_target_pairs={{0,1},{1,2},{2,3},{3,0},{4,5},{5,6},{6,7},{7,4},{8,9},{9,10},{10,1... | collective-permute-start | bytes 393224 | tf_op jit(solution)/shard_map/ppermute | solution.py:83
  69.2 51.4 %collective-permute-start.31 = (bf16[64,1024]{1,0:T(8,128)(2,1)S(1)}, bf16[64,1024]{1,0:T(8,128)(2,1)S(1)}, u32[]{:S(2)}, u32[]{:S(2)}) collective-permute-start(bf16[64,1024]{1,0:T(8,128)(2,1)S(1)} %get-tuple-element.82), channel_id=1, source_target_pairs={{0,2},{1,3},{2,0},{3,1},{4,6},{5,7},{6,4},{7,5},{8,10},{9,11},{10,... | collective-permute-start | bytes 393224 | tf_op jit(solution)/shard_map/ppermute | solution.py:83
  71.6 49.4 %collective-permute-start.32 = (bf16[64,1024]{1,0:T(8,128)(2,1)S(1)}, bf16[64,1024]{1,0:T(8,128)(2,1)S(1)}, u32[]{:S(2)}, u32[]{:S(2)}) collective-permute-start(bf16[64,1024]{1,0:T(8,128)(2,1)S(1)} %get-tuple-element.82), channel_id=1, source_target_pairs={{0,3},{1,0},{2,1},{3,2},{4,7},{5,4},{6,5},{7,6},{8,11},{9,8},{10,9... | collective-permute-start | bytes 393224 | tf_op jit(solution)/shard_map/ppermute | solution.py:83
  103.5 27.9 %collective-permute-start.1 = (bf16[1024,1024]{0,1:T(8,128)(2,1)}, bf16[1024,1024]{0,1:T(8,128)(2,1)S(1)}, u32[]{:S(2)}, u32[]{:S(2)}) collective-permute-start(bf16[1024,1024]{0,1:T(8,128)(2,1)} %bitcast.288), channel_id=1, source_target_pairs={{0,16},{16,0},{1,17},{17,1},{2,18},{18,2},{3,19},{19,3},{4,20},{20... | collective-permute-start | bytes 6291464 | tf_op jit(solution)/shard_map/ppermute | solution.py:66
  119.8 62.3 %collective-permute-start.8 = (bf16[1024,1024]{0,1:T(8,128)(2,1)}, bf16[1024,1024]{0,1:T(8,128)(2,1)}, u32[]{:S(2)}, u32[]{:S(2)}) collective-permute-start(bf16[1024,1024]{0,1:T(8,128)(2,1)} %bitcast.295), channel_id=1, source_target_pairs={{0,16},{16,0},{1,17},{17,1},{2,18},{18,2},{3,19},{19,3},{4,20},{20... | collective-permute-start | bytes 6291464 | tf_op jit(solution)/shard_map/ppermute | solution.py:66
  120.6 66.3 %collective-permute-start.9 = (bf16[1024,1024]{0,1:T(8,128)(2,1)}, bf16[1024,1024]{0,1:T(8,128)(2,1)}, u32[]{:S(2)}, u32[]{:S(2)}) collective-permute-start(bf16[1024,1024]{0,1:T(8,128)(2,1)} %bitcast.300), channel_id=1, source_target_pairs={{0,16},{16,0},{1,17},{17,1},{2,18},{18,2},{3,19},{19,3},{4,20},{20... | collective-permute-start | bytes 6291464 | tf_op jit(solution)/shard_map/ppermute | solution.py:66
  136.5 8.6 %collective-permute-start.2 = (bf16[64,1152]{1,0:T(8,128)(2,1)S(1)}, bf16[64,1152]{1,0:T(8,128)(2,1)S(1)}, u32[]{:S(2)}, u32[]{:S(2)}) collective-permute-start(bf16[64,1152]{1,0:T(8,128)(2,1)S(1)} %concatenate.110), channel_id=1, source_target_pairs={{0,1},{1,2},{2,3},{3,0},{4,5},{5,6},{6,7},{7,4},{8,9},{9,10},{10,1... | collective-permute-start | bytes 442376 | tf_op jit(solution)/shard_map/ppermute | solution.py:83
  138.0 12.6 %collective-permute-start.3 = (bf16[64,1152]{1,0:T(8,128)(2,1)S(1)}, bf16[64,1152]{1,0:T(8,128)(2,1)S(1)}, u32[]{:S(2)}, u32[]{:S(2)}) collective-permute-start(bf16[64,1152]{1,0:T(8,128)(2,1)S(1)} %concatenate.110), channel_id=1, source_target_pairs={{0,2},{1,3},{2,0},{3,1},{4,6},{5,7},{6,4},{7,5},{8,10},{9,11},{10,... | collective-permute-start | bytes 442376 | tf_op jit(solution)/shard_map/ppermute | solution.py:83
  140.4 10.2 %collective-permute-start.4 = (bf16[64,1152]{1,0:T(8,128)(2,1)S(1)}, bf16[64,1152]{1,0:T(8,128)(2,1)S(1)}, u32[]{:S(2)}, u32[]{:S(2)}) collective-permute-start(bf16[64,1152]{1,0:T(8,128)(2,1)S(1)} %concatenate.110), channel_id=1, source_target_pairs={{0,3},{1,0},{2,1},{3,2},{4,7},{5,4},{6,5},{7,6},{8,11},{9,8},{10,9... | collective-permute-start | bytes 442376 | tf_op jit(solution)/shard_map/ppermute | solution.py:83
  150.7 16.3 %collective-permute-start.5 = (bf16[256,1152]{1,0:T(8,128)(2,1)S(1)}, bf16[256,1152]{1,0:T(8,128)(2,1)S(1)}, u32[]{:S(2)}, u32[]{:S(2)}) collective-permute-start(bf16[256,1152]{1,0:T(8,128)(2,1)S(1)} %pad_maximum_fusion.3), channel_id=1, source_target_pairs={{0,4},{4,0},{8,12},{12,8},{1,5},{5,1},{9,13},{13,9},{2,6},{6,2},{1... | collective-permute-start | bytes 1769480 | tf_op jit(solution)/shard_map/ppermute | solution.py:87
  152.2 26.7 %collective-permute-start.6 = (bf16[256,1152]{1,0:T(8,128)(2,1)S(1)}, bf16[256,1152]{1,0:T(8,128)(2,1)S(1)}, u32[]{:S(2)}, u32[]{:S(2)}) collective-permute-start(bf16[256,1152]{1,0:T(8,128)(2,1)S(1)} %pad_maximum_fusion.3), channel_id=1, source_target_pairs={{0,8},{4,12},{8,0},{12,4},{1,9},{5,13},{9,1},{13,5},{2,10},{6,14},... | collective-permute-start | bytes 1769480 | tf_op jit(solution)/shard_map/ppermute | solution.py:87
  152.8 27.8 %collective-permute-start.7 = (bf16[256,1152]{1,0:T(8,128)(2,1)S(1)}, bf16[256,1152]{1,0:T(8,128)(2,1)S(1)}, u32[]{:S(2)}, u32[]{:S(2)}) collective-permute-start(bf16[256,1152]{1,0:T(8,128)(2,1)S(1)} %pad_maximum_fusion.3), channel_id=1, source_target_pairs={{0,12},{4,8},{8,4},{12,0},{1,13},{5,9},{9,5},{13,1},{2,14},{6,10},... | collective-permute-start | bytes 1769480 | tf_op jit(solution)/shard_map/ppermute | solution.py:87
  167.0 24.7 %collective-permute-start.10 = (bf16[1024,1024]{0,1:T(8,128)(2,1)S(1)}, bf16[1024,1024]{0,1:T(8,128)(2,1)S(1)}, u32[]{:S(2)}, u32[]{:S(2)}) collective-permute-start(bf16[1024,1024]{0,1:T(8,128)(2,1)S(1)} %copy-done.23), channel_id=1, source_target_pairs={{0,16},{16,0},{1,17},{17,1},{2,18},{18,2},{3,19},{19,3},{4,20},{20... | collective-permute-start | bytes 6291464 | tf_op jit(solution)/shard_map/ppermute | solution.py:66
  178.9 17.4 %collective-permute-start.33 = (bf16[256,1024]{1,0:T(8,128)(2,1)}, bf16[256,1024]{1,0:T(8,128)(2,1)S(1)}, u32[]{:S(2)}, u32[]{:S(2)}) collective-permute-start(bf16[256,1024]{1,0:T(8,128)(2,1)} %pad_maximum_fusion.5), channel_id=1, source_target_pairs={{0,4},{4,0},{8,12},{12,8},{1,5},{5,1},{9,13},{13,9},{2,6},{6,2},{1... | collective-permute-start | bytes 1572872 | tf_op jit(solution)/shard_map/ppermute | solution.py:87
  180.6 24.5 %collective-permute-start.34 = (bf16[256,1024]{1,0:T(8,128)(2,1)S(1)}, bf16[256,1024]{1,0:T(8,128)(2,1)S(1)}, u32[]{:S(2)}, u32[]{:S(2)}) collective-permute-start(bf16[256,1024]{1,0:T(8,128)(2,1)S(1)} %copy-done.55), channel_id=1, source_target_pairs={{0,8},{4,12},{8,0},{12,4},{1,9},{5,13},{9,1},{13,5},{2,10},{6,14},... | collective-permute-start | bytes 1572872 | tf_op jit(solution)/shard_map/ppermute | solution.py:87
  182.1 23.0 %collective-permute-start.35 = (bf16[256,1024]{1,0:T(8,128)(2,1)S(1)}, bf16[256,1024]{1,0:T(8,128)(2,1)S(1)}, u32[]{:S(2)}, u32[]{:S(2)}) collective-permute-start(bf16[256,1024]{1,0:T(8,128)(2,1)S(1)} %copy-done.55), channel_id=1, source_target_pairs={{0,12},{4,8},{8,4},{12,0},{1,13},{5,9},{9,5},{13,1},{2,14},{6,10},... | collective-permute-start | bytes 1572872 | tf_op jit(solution)/shard_map/ppermute | solution.py:87
  194.2 19.5 %collective-permute-start.11 = (bf16[256,1024]{1,0:T(8,128)(2,1)S(1)}, bf16[256,1024]{1,0:T(8,128)(2,1)S(1)}, u32[]{:S(2)}, u32[]{:S(2)}) collective-permute-start(bf16[256,1024]{1,0:T(8,128)(2,1)S(1)} %get-tuple-element.104), channel_id=1, source_target_pairs={{0,4},{4,0},{8,12},{12,8},{1,5},{5,1},{9,13},{13,9},{2,6},{6,2},{1... | collective-permute-start | bytes 1572872 | tf_op jit(solution)/shard_map/ppermute | solution.py:95
  195.7 30.4 %collective-permute-start.12 = (bf16[256,1024]{1,0:T(8,128)(2,1)S(1)}, bf16[256,1024]{1,0:T(8,128)(2,1)S(1)}, u32[]{:S(2)}, u32[]{:S(2)}) collective-permute-start(bf16[256,1024]{1,0:T(8,128)(2,1)S(1)} %get-tuple-element.106), channel_id=1, source_target_pairs={{0,8},{4,12},{8,0},{12,4},{1,9},{5,13},{9,1},{13,5},{2,10},{6,14},... | collective-permute-start | bytes 1572872 | tf_op jit(solution)/shard_map/ppermute | solution.py:95
  196.3 29.9 %collective-permute-start.13 = (bf16[256,1024]{1,0:T(8,128)(2,1)S(1)}, bf16[256,1024]{1,0:T(8,128)(2,1)S(1)}, u32[]{:S(2)}, u32[]{:S(2)}) collective-permute-start(bf16[256,1024]{1,0:T(8,128)(2,1)S(1)} %get-tuple-element.105), channel_id=1, source_target_pairs={{0,12},{4,8},{8,4},{12,0},{1,13},{5,9},{9,5},{13,1},{2,14},{6,10},... | collective-permute-start | bytes 1572872 | tf_op jit(solution)/shard_map/ppermute | solution.py:95
  226.5 10.0 %collective-permute-start.14 = (bf16[64,1024]{1,0:T(8,128)(2,1)S(1)}, bf16[64,1024]{1,0:T(8,128)(2,1)S(1)}, u32[]{:S(2)}, u32[]{:S(2)}) collective-permute-start(bf16[64,1024]{1,0:T(8,128)(2,1)S(1)} %get-tuple-element.130), channel_id=1, source_target_pairs={{0,3},{1,0},{2,1},{3,2},{4,7},{5,4},{6,5},{7,6},{8,11},{9,8},{10,9... | collective-permute-start | bytes 393224 | tf_op jit(solution)/shard_map/ppermute | solution.py:99
  230.3 12.0 %collective-permute-start.15 = (bf16[64,1024]{1,0:T(8,128)(2,1)S(1)}, bf16[64,1024]{1,0:T(8,128)(2,1)S(1)}, u32[]{:S(2)}, u32[]{:S(2)}) collective-permute-start(bf16[64,1024]{1,0:T(8,128)(2,1)S(1)} %get-tuple-element.132), channel_id=1, source_target_pairs={{0,2},{1,3},{2,0},{3,1},{4,6},{5,7},{6,4},{7,5},{8,10},{9,11},{10,... | collective-permute-start | bytes 393224 | tf_op jit(solution)/shard_map/ppermute | solution.py:99
  231.9 10.3 %collective-permute-start.16 = (bf16[64,1024]{1,0:T(8,128)(2,1)S(1)}, bf16[64,1024]{1,0:T(8,128)(2,1)S(1)}, u32[]{:S(2)}, u32[]{:S(2)}) collective-permute-start(bf16[64,1024]{1,0:T(8,128)(2,1)S(1)} %get-tuple-element.131), channel_id=1, source_target_pairs={{0,1},{1,2},{2,3},{3,0},{4,5},{5,6},{6,7},{7,4},{8,9},{9,10},{10,1... | collective-permute-start | bytes 393224 | tf_op jit(solution)/shard_map/ppermute | solution.py:99
  262.8 10.7 %collective-permute-start.18 = (bf16[64,1152]{1,0:T(8,128)(2,1)S(1)}, bf16[64,1152]{1,0:T(8,128)(2,1)S(1)}, u32[]{:S(2)}, u32[]{:S(2)}) collective-permute-start(bf16[64,1152]{1,0:T(8,128)(2,1)S(1)} %concatenate.117), channel_id=1, source_target_pairs={{0,2},{1,3},{2,0},{3,1},{4,6},{5,7},{6,4},{7,5},{8,10},{9,11},{10,... | collective-permute-start | bytes 442376 | tf_op jit(solution)/shard_map/ppermute | solution.py:83
  263.8 9.7 %collective-permute-start.19 = (bf16[64,1152]{1,0:T(8,128)(2,1)S(1)}, bf16[64,1152]{1,0:T(8,128)(2,1)S(1)}, u32[]{:S(2)}, u32[]{:S(2)}) collective-permute-start(bf16[64,1152]{1,0:T(8,128)(2,1)S(1)} %concatenate.117), channel_id=1, source_target_pairs={{0,3},{1,0},{2,1},{3,2},{4,7},{5,4},{6,5},{7,6},{8,11},{9,8},{10,9... | collective-permute-start | bytes 442376 | tf_op jit(solution)/shard_map/ppermute | solution.py:83
  273.5 15.2 %collective-permute-start.20 = (bf16[256,1152]{1,0:T(8,128)(2,1)S(1)}, bf16[256,1152]{1,0:T(8,128)(2,1)S(1)}, u32[]{:S(2)}, u32[]{:S(2)}) collective-permute-start(bf16[256,1152]{1,0:T(8,128)(2,1)S(1)} %pad_maximum_fusion.4), channel_id=1, source_target_pairs={{0,4},{4,0},{8,12},{12,8},{1,5},{5,1},{9,13},{13,9},{2,6},{6,2},{1... | collective-permute-start | bytes 1769480 | tf_op jit(solution)/shard_map/ppermute | solution.py:87
  274.2 21.1 %collective-permute-start.21 = (bf16[256,1152]{1,0:T(8,128)(2,1)S(1)}, bf16[256,1152]{1,0:T(8,128)(2,1)S(1)}, u32[]{:S(2)}, u32[]{:S(2)}) collective-permute-start(bf16[256,1152]{1,0:T(8,128)(2,1)S(1)} %pad_maximum_fusion.4), channel_id=1, source_target_pairs={{0,8},{4,12},{8,0},{12,4},{1,9},{5,13},{9,1},{13,5},{2,10},{6,14},... | collective-permute-start | bytes 1769480 | tf_op jit(solution)/shard_map/ppermute | solution.py:87
  275.6 19.7 %collective-permute-start.22 = (bf16[256,1152]{1,0:T(8,128)(2,1)S(1)}, bf16[256,1152]{1,0:T(8,128)(2,1)S(1)}, u32[]{:S(2)}, u32[]{:S(2)}) collective-permute-start(bf16[256,1152]{1,0:T(8,128)(2,1)S(1)} %pad_maximum_fusion.4), channel_id=1, source_target_pairs={{0,12},{4,8},{8,4},{12,0},{1,13},{5,9},{9,5},{13,1},{2,14},{6,10},... | collective-permute-start | bytes 1769480 | tf_op jit(solution)/shard_map/ppermute | solution.py:87
  320.8 16.7 %collective-permute-start.23 = (bf16[256,1024]{1,0:T(8,128)(2,1)S(1)}, bf16[256,1024]{1,0:T(8,128)(2,1)S(1)}, u32[]{:S(2)}, u32[]{:S(2)}) collective-permute-start(bf16[256,1024]{1,0:T(8,128)(2,1)S(1)} %get-tuple-element.101), channel_id=1, source_target_pairs={{0,4},{4,0},{8,12},{12,8},{1,5},{5,1},{9,13},{13,9},{2,6},{6,2},{1... | collective-permute-start | bytes 1572872 | tf_op jit(solution)/shard_map/ppermute | solution.py:95
  322.3 26.0 %collective-permute-start.24 = (bf16[256,1024]{1,0:T(8,128)(2,1)S(1)}, bf16[256,1024]{1,0:T(8,128)(2,1)S(1)}, u32[]{:S(2)}, u32[]{:S(2)}) collective-permute-start(bf16[256,1024]{1,0:T(8,128)(2,1)S(1)} %get-tuple-element.103), channel_id=1, source_target_pairs={{0,8},{4,12},{8,0},{12,4},{1,9},{5,13},{9,1},{13,5},{2,10},{6,14},... | collective-permute-start | bytes 1572872 | tf_op jit(solution)/shard_map/ppermute | solution.py:95
  322.9 25.4 %collective-permute-start.25 = (bf16[256,1024]{1,0:T(8,128)(2,1)S(1)}, bf16[256,1024]{1,0:T(8,128)(2,1)S(1)}, u32[]{:S(2)}, u32[]{:S(2)}) collective-permute-start(bf16[256,1024]{1,0:T(8,128)(2,1)S(1)} %get-tuple-element.102), channel_id=1, source_target_pairs={{0,12},{4,8},{8,4},{12,0},{1,13},{5,9},{9,5},{13,1},{2,14},{6,10},... | collective-permute-start | bytes 1572872 | tf_op jit(solution)/shard_map/ppermute | solution.py:95
  335.4 18.7 %collective-permute-start.36 = (bf16[256,1152]{1,0:T(8,128)(2,1)S(1)}, bf16[256,1152]{1,0:T(8,128)(2,1)S(1)}, u32[]{:S(2)}, u32[]{:S(2)}) collective-permute-start(bf16[256,1152]{1,0:T(8,128)(2,1)S(1)} %get-tuple-element.98), channel_id=1, source_target_pairs={{0,4},{4,0},{8,12},{12,8},{1,5},{5,1},{9,13},{13,9},{2,6},{6,2},{1... | collective-permute-start | bytes 1769480 | tf_op jit(solution)/shard_map/ppermute | solution.py:95
  336.9 24.5 %collective-permute-start.37 = (bf16[256,1152]{1,0:T(8,128)(2,1)S(1)}, bf16[256,1152]{1,0:T(8,128)(2,1)S(1)}, u32[]{:S(2)}, u32[]{:S(2)}) collective-permute-start(bf16[256,1152]{1,0:T(8,128)(2,1)S(1)} %get-tuple-element.100), channel_id=1, source_target_pairs={{0,8},{4,12},{8,0},{12,4},{1,9},{5,13},{9,1},{13,5},{2,10},{6,14},... | collective-permute-start | bytes 1769480 | tf_op jit(solution)/shard_map/ppermute | solution.py:95
  337.5 24.0 %collective-permute-start.38 = (bf16[256,1152]{1,0:T(8,128)(2,1)S(1)}, bf16[256,1152]{1,0:T(8,128)(2,1)S(1)}, u32[]{:S(2)}, u32[]{:S(2)}) collective-permute-start(bf16[256,1152]{1,0:T(8,128)(2,1)S(1)} %get-tuple-element.99), channel_id=1, source_target_pairs={{0,12},{4,8},{8,4},{12,0},{1,13},{5,9},{9,5},{13,1},{2,14},{6,10},... | collective-permute-start | bytes 1769480 | tf_op jit(solution)/shard_map/ppermute | solution.py:95
  361.8 17.6 %collective-permute-start.39 = (bf16[64,1152]{1,0:T(8,128)(2,1)S(1)}, bf16[64,1152]{1,0:T(8,128)(2,1)S(1)}, u32[]{:S(2)}, u32[]{:S(2)}) collective-permute-start(bf16[64,1152]{1,0:T(8,128)(2,1)S(1)} %get-tuple-element.112), channel_id=1, source_target_pairs={{0,3},{1,0},{2,1},{3,2},{4,7},{5,4},{6,5},{7,6},{8,11},{9,8},{10,9... | collective-permute-start | bytes 442376 | tf_op jit(solution)/shard_map/ppermute | solution.py:99
  373.7 15.1 %collective-permute-start.40 = (bf16[64,1152]{1,0:T(8,128)(2,1)S(1)}, bf16[64,1152]{1,0:T(8,128)(2,1)S(1)}, u32[]{:S(2)}, u32[]{:S(2)}) collective-permute-start(bf16[64,1152]{1,0:T(8,128)(2,1)S(1)} %get-tuple-element.114), channel_id=1, source_target_pairs={{0,2},{1,3},{2,0},{3,1},{4,6},{5,7},{6,4},{7,5},{8,10},{9,11},{10,... | collective-permute-start | bytes 442376 | tf_op jit(solution)/shard_map/ppermute | solution.py:99
  374.7 14.1 %collective-permute-start.41 = (bf16[64,1152]{1,0:T(8,128)(2,1)S(1)}, bf16[64,1152]{1,0:T(8,128)(2,1)S(1)}, u32[]{:S(2)}, u32[]{:S(2)}) collective-permute-start(bf16[64,1152]{1,0:T(8,128)(2,1)S(1)} %get-tuple-element.113), channel_id=1, source_target_pairs={{0,1},{1,2},{2,3},{3,0},{4,5},{5,6},{6,7},{7,4},{8,9},{9,10},{10,1... | collective-permute-start | bytes 442376 | tf_op jit(solution)/shard_map/ppermute | solution.py:99
  375.6 35.5 %collective-permute-start.26 = (bf16[64,1024]{1,0:T(8,128)(2,1)}, bf16[64,1024]{1,0:T(8,128)(2,1)}, u32[]{:S(2)}, u32[]{:S(2)}) collective-permute-start(bf16[64,1024]{1,0:T(8,128)(2,1)} %get-tuple-element.127), channel_id=1, source_target_pairs={{0,3},{1,0},{2,1},{3,2},{4,7},{5,4},{6,5},{7,6},{8,11},{9,8},{10,9... | collective-permute-start | bytes 393224 | tf_op jit(solution)/shard_map/ppermute | solution.py:99
  379.3 31.9 %collective-permute-start.27 = (bf16[64,1024]{1,0:T(8,128)(2,1)}, bf16[64,1024]{1,0:T(8,128)(2,1)}, u32[]{:S(2)}, u32[]{:S(2)}) collective-permute-start(bf16[64,1024]{1,0:T(8,128)(2,1)} %get-tuple-element.129), channel_id=1, source_target_pairs={{0,2},{1,3},{2,0},{3,1},{4,6},{5,7},{6,4},{7,5},{8,10},{9,11},{10,... | collective-permute-start | bytes 393224 | tf_op jit(solution)/shard_map/ppermute | solution.py:99
  379.4 31.7 %collective-permute-start.28 = (bf16[64,1024]{1,0:T(8,128)(2,1)}, bf16[64,1024]{1,0:T(8,128)(2,1)}, u32[]{:S(2)}, u32[]{:S(2)}) collective-permute-start(bf16[64,1024]{1,0:T(8,128)(2,1)} %get-tuple-element.128), channel_id=1, source_target_pairs={{0,1},{1,2},{2,3},{3,0},{4,5},{5,6},{6,7},{7,4},{8,9},{9,10},{10,1... | collective-permute-start | bytes 393224 | tf_op jit(solution)/shard_map/ppermute | solution.py:99
  413.3 8.7 %collective-permute-start.43 = (bf16[64,1024]{1,0:T(8,128)(2,1)S(1)}, bf16[64,1024]{1,0:T(8,128)(2,1)S(1)}, u32[]{:S(2)}, u32[]{:S(2)}) collective-permute-start(bf16[64,1024]{1,0:T(8,128)(2,1)S(1)} %get-tuple-element.79), channel_id=1, source_target_pairs={{0,2},{1,3},{2,0},{3,1},{4,6},{5,7},{6,4},{7,5},{8,10},{9,11},{10,... | collective-permute-start | bytes 393224 | tf_op jit(solution)/shard_map/ppermute | solution.py:83
  422.0 9.2 %collective-permute-start.45 = (bf16[256,1024]{1,0:T(8,128)(2,1)S(1)}, bf16[256,1024]{1,0:T(8,128)(2,1)S(1)}, u32[]{:S(2)}, u32[]{:S(2)}) collective-permute-start(bf16[256,1024]{1,0:T(8,128)(2,1)S(1)} %pad_maximum_fusion.7), channel_id=1, source_target_pairs={{0,4},{4,0},{8,12},{12,8},{1,5},{5,1},{9,13},{13,9},{2,6},{6,2},{1... | collective-permute-start | bytes 1572872 | tf_op jit(solution)/shard_map/ppermute | solution.py:87
  422.7 14.8 %collective-permute-start.46 = (bf16[256,1024]{1,0:T(8,128)(2,1)S(1)}, bf16[256,1024]{1,0:T(8,128)(2,1)S(1)}, u32[]{:S(2)}, u32[]{:S(2)}) collective-permute-start(bf16[256,1024]{1,0:T(8,128)(2,1)S(1)} %pad_maximum_fusion.7), channel_id=1, source_target_pairs={{0,8},{4,12},{8,0},{12,4},{1,9},{5,13},{9,1},{13,5},{2,10},{6,14},... | collective-permute-start | bytes 1572872 | tf_op jit(solution)/shard_map/ppermute | solution.py:87
  424.1 13.4 %collective-permute-start.47 = (bf16[256,1024]{1,0:T(8,128)(2,1)S(1)}, bf16[256,1024]{1,0:T(8,128)(2,1)S(1)}, u32[]{:S(2)}, u32[]{:S(2)}) collective-permute-start(bf16[256,1024]{1,0:T(8,128)(2,1)S(1)} %pad_maximum_fusion.7), channel_id=1, source_target_pairs={{0,12},{4,8},{8,4},{12,0},{1,13},{5,9},{9,5},{13,1},{2,14},{6,10},... | collective-permute-start | bytes 1572872 | tf_op jit(solution)/shard_map/ppermute | solution.py:87
  454.9 13.7 %collective-permute-start.48 = (bf16[256,1152]{1,0:T(8,128)(2,1)}, bf16[256,1152]{1,0:T(8,128)(2,1)}, u32[]{:S(2)}, u32[]{:S(2)}) collective-permute-start(bf16[256,1152]{1,0:T(8,128)(2,1)} %get-tuple-element.95), channel_id=1, source_target_pairs={{0,4},{4,0},{8,12},{12,8},{1,5},{5,1},{9,13},{13,9},{2,6},{6,2},{1... | collective-permute-start | bytes 1769480 | tf_op jit(solution)/shard_map/ppermute | solution.py:95
  456.3 16.6 %collective-permute-start.49 = (bf16[256,1152]{1,0:T(8,128)(2,1)}, bf16[256,1152]{1,0:T(8,128)(2,1)}, u32[]{:S(2)}, u32[]{:S(2)}) collective-permute-start(bf16[256,1152]{1,0:T(8,128)(2,1)} %get-tuple-element.97), channel_id=1, source_target_pairs={{0,8},{4,12},{8,0},{12,4},{1,9},{5,13},{9,1},{13,5},{2,10},{6,14},... | collective-permute-start | bytes 1769480 | tf_op jit(solution)/shard_map/ppermute | solution.py:95
  456.9 16.0 %collective-permute-start.50 = (bf16[256,1152]{1,0:T(8,128)(2,1)}, bf16[256,1152]{1,0:T(8,128)(2,1)}, u32[]{:S(2)}, u32[]{:S(2)}) collective-permute-start(bf16[256,1152]{1,0:T(8,128)(2,1)} %get-tuple-element.96), channel_id=1, source_target_pairs={{0,12},{4,8},{8,4},{12,0},{1,13},{5,9},{9,5},{13,1},{2,14},{6,10},... | collective-permute-start | bytes 1769480 | tf_op jit(solution)/shard_map/ppermute | solution.py:95
  475.5 21.7 %collective-permute-start.51 = (bf16[64,1152]{1,0:T(8,128)(2,1)}, bf16[64,1152]{1,0:T(8,128)(2,1)}, u32[]{:S(2)}, u32[]{:S(2)}) collective-permute-start(bf16[64,1152]{1,0:T(8,128)(2,1)} %get-tuple-element.109), channel_id=1, source_target_pairs={{0,3},{1,0},{2,1},{3,2},{4,7},{5,4},{6,5},{7,6},{8,11},{9,8},{10,9... | collective-permute-start | bytes 442376 | tf_op jit(solution)/shard_map/ppermute | solution.py:99
  479.3 17.9 %collective-permute-start.52 = (bf16[64,1152]{1,0:T(8,128)(2,1)}, bf16[64,1152]{1,0:T(8,128)(2,1)}, u32[]{:S(2)}, u32[]{:S(2)}) collective-permute-start(bf16[64,1152]{1,0:T(8,128)(2,1)} %get-tuple-element.111), channel_id=1, source_target_pairs={{0,2},{1,3},{2,0},{3,1},{4,6},{5,7},{6,4},{7,5},{8,10},{9,11},{10,... | collective-permute-start | bytes 442376 | tf_op jit(solution)/shard_map/ppermute | solution.py:99
  479.3 17.9 %collective-permute-start.53 = (bf16[64,1152]{1,0:T(8,128)(2,1)}, bf16[64,1152]{1,0:T(8,128)(2,1)}, u32[]{:S(2)}, u32[]{:S(2)}) collective-permute-start(bf16[64,1152]{1,0:T(8,128)(2,1)} %get-tuple-element.110), channel_id=1, source_target_pairs={{0,1},{1,2},{2,3},{3,0},{4,5},{5,6},{6,7},{7,4},{8,9},{9,10},{10,1... | collective-permute-start | bytes 442376 | tf_op jit(solution)/shard_map/ppermute | solution.py:99
  493.2 47.0 %collective-permute-start.56 = (bf16[1024,3200]{1,0:T(8,128)(2,1)}, bf16[1024,3200]{1,0:T(8,128)(2,1)}, u32[]{:S(2)}, u32[]{:S(2)}) collective-permute-start(bf16[1024,3200]{1,0:T(8,128)(2,1)} %concatenate.133), channel_id=1, source_target_pairs={{0,16},{1,17},{2,18},{3,19},{4,20},{5,21},{6,22},{7,23},{8,24},{9,... | collective-permute-start | bytes 19660808 | tf_op jit(solution)/shard_map/ppermute | solution.py:396
  538.9 12.6 %collective-permute-start.55 = (bf16[1024,3200]{1,0:T(8,128)(2,1)}, bf16[1024,3200]{1,0:T(8,128)(2,1)S(1)}, u32[]{:S(2)}, u32[]{:S(2)}) collective-permute-start(bf16[1024,3200]{1,0:T(8,128)(2,1)} %concatenate.132), channel_id=1, source_target_pairs={{16,0},{17,1},{18,2},{19,3},{20,4},{21,5},{22,6},{23,7},{24,8},{25... | collective-permute-start | bytes 19660808 | tf_op jit(solution)/shard_map/ppermute | solution.py:396
  562.7 146.0 %all-reduce.2.cloned.1.call-start = ((), (), s32[]{:S(2)}) async-start(), calls=%async_computation.3 | async-start | bytes 3276800 | tf_op jit(solution)/shard_map/psum | solution.py:407
  569.6 30.3 %collective-permute-start.62 = (bf16[1024,1024]{0,1:T(8,128)(2,1)S(1)}, bf16[1024,1024]{0,1:T(8,128)(2,1)S(1)}, u32[]{:S(2)}, u32[]{:S(2)}) collective-permute-start(bf16[1024,1024]{0,1:T(8,128)(2,1)S(1)} %convolution_convert_fusion.2), channel_id=1, source_target_pairs={{0,16},{1,17},{2,18},{3,19},{4,20},{5,21},{6,22},{7,23},{8,24},{9,... | collective-permute-start | bytes 6291464 | tf_op jit(solution)/shard_map/ppermute | solution.py:396
  576.1 72.7 %collective-permute-start.60 = (bf16[1024,1024]{0,1:T(8,128)(2,1)}, bf16[1024,1024]{0,1:T(8,128)(2,1)}, u32[]{:S(2)}, u32[]{:S(2)}) collective-permute-start(bf16[1024,1024]{0,1:T(8,128)(2,1)} %convolution_convert_fusion.4), channel_id=1, source_target_pairs={{0,16},{1,17},{2,18},{3,19},{4,20},{5,21},{6,22},{7,23},{8,24},{9,... | collective-permute-start | bytes 6291464 | tf_op jit(solution)/shard_map/ppermute | solution.py:396
  581.4 11.0 %collective-permute-start.29 = (bf16[64,1024]{1,0:T(8,128)(2,1)S(1)}, bf16[64,1024]{1,0:T(8,128)(2,1)S(1)}, u32[]{:S(2)}, u32[]{:S(2)}) collective-permute-start(bf16[64,1024]{1,0:T(8,128)(2,1)S(1)} %copy-done.82), channel_id=1, source_target_pairs={{0,16},{16,0},{1,17},{17,1},{2,18},{18,2},{3,19},{19,3},{4,20},{20... | collective-permute-start | bytes 393224 | tf_op jit(solution)/shard_map/ppermute | solution.py:411
  585.3 50.7 %collective-permute-start.61 = (bf16[1024,1024]{0,1:T(8,128)(2,1)}, bf16[1024,1024]{0,1:T(8,128)(2,1)}, u32[]{:S(2)}, u32[]{:S(2)}) collective-permute-start(bf16[1024,1024]{0,1:T(8,128)(2,1)} %convolution_convert_fusion.3), channel_id=1, source_target_pairs={{16,0},{17,1},{18,2},{19,3},{20,4},{21,5},{22,6},{23,7},{24,8},{25... | collective-permute-start | bytes 6291464 | tf_op jit(solution)/shard_map/ppermute | solution.py:396
  590.7 58.1 %collective-permute-start.59 = (bf16[1024,1024]{0,1:T(8,128)(2,1)}, bf16[1024,1024]{0,1:T(8,128)(2,1)}, u32[]{:S(2)}, u32[]{:S(2)}) collective-permute-start(bf16[1024,1024]{0,1:T(8,128)(2,1)} %convolution_convert_fusion.5), channel_id=1, source_target_pairs={{16,0},{17,1},{18,2},{19,3},{20,4},{21,5},{22,6},{23,7},{24,8},{25... | collective-permute-start | bytes 6291464 | tf_op jit(solution)/shard_map/ppermute | solution.py:396
  592.4 10.9 %collective-permute-start.54 = (bf16[64,1024]{1,0:T(8,128)(2,1)S(1)}, bf16[64,1024]{1,0:T(8,128)(2,1)S(1)}, u32[]{:S(2)}, u32[]{:S(2)}) collective-permute-start(bf16[64,1024]{1,0:T(8,128)(2,1)S(1)} %select_convert_fusion.1), channel_id=1, source_target_pairs={{0,16},{16,0},{1,17},{17,1},{2,18},{18,2},{3,19},{19,3},{4,20},{20... | collective-permute-start | bytes 393224 | tf_op jit(solution)/shard_map/ppermute | solution.py:411
  599.9 61.6 %collective-permute-start.58 = (bf16[1024,1024]{0,1:T(8,128)(2,1)S(1)}, bf16[1024,1024]{0,1:T(8,128)(2,1)}, u32[]{:S(2)}, u32[]{:S(2)}) collective-permute-start(bf16[1024,1024]{0,1:T(8,128)(2,1)S(1)} %convolution_convert_fusion.6), channel_id=1, source_target_pairs={{0,16},{1,17},{2,18},{3,19},{4,20},{5,21},{6,22},{7,23},{8,24},{9,... | collective-permute-start | bytes 6291464 | tf_op jit(solution)/shard_map/ppermute | solution.py:396
  603.3 58.3 %collective-permute-start.57 = (bf16[1024,1024]{0,1:T(8,128)(2,1)}, bf16[1024,1024]{0,1:T(8,128)(2,1)}, u32[]{:S(2)}, u32[]{:S(2)}) collective-permute-start(bf16[1024,1024]{0,1:T(8,128)(2,1)} %convolution_convert_fusion.7), channel_id=1, source_target_pairs={{16,0},{17,1},{18,2},{19,3},{20,4},{21,5},{22,6},{23,7},{24,8},{25... | collective-permute-start | bytes 6291464 | tf_op jit(solution)/shard_map/ppermute | solution.py:396
  (148 other events, 1980.9 us)
Sparse Core Ops, SparseCore 0:
  10.5 55.3 all-gather.5
  68.3 35.2 all-gather.7
  562.8 72.3 reduce-scatter.1
  637.4 71.2 all-reduce.1
